TPU v7x, 256 devices: a whole 4x4x8 slice. The times are simulated.
256 devices in a mesh: gx: 32 (over x, z), gy: 8 (over y, core).
Axes of the slice: x: 4, y: 4, z: 8, core: 2. Of those that a mesh axis runs over, the one named last changes fastest.
Arguments:
- right_sides: float32 [16, 32, 128, 1024], P(None, None, 'gx', 'gy'), may hold values from -2000 to 2000
- region_labels: int32 [32, 128, 1024], P(None, 'gx', 'gy'), may hold values from 0 to 7
- face_flags: int32 [2, 128, 1024], P(None, 'gx', 'gy'), may hold values 0 or 1
- region_perm: float32 [8], replicated, may hold values from 0.1 to 10
Outputs:
- orthonormal: float32 [80, 32, 128, 1024], P(None, None, 'gx', 'gy')
- triangular_factor: float32 [80, 80], replicated
All inputs are finite; a program needn't handle non-finite values. No bound on the sum of `face_flags` on one device may be relied on, other than what follows from the above.
Results may differ from a plain program's by a relative error of at most 0.0003.
Values sent between devices are 32-bit elements; how exact they have to be, the bound alone decides.
A program may use at most 128 MiB of HBM per device.

v0:
```python
import functools
import jax
import jax.numpy as jnp
from jax import lax
from jax.experimental import pallas as pl
from jax.experimental.pallas import tpu as pltpu
from jax.sharding import PartitionSpec as P

RHS = 16
S = 4
VECS = S + 1
COLS = RHS * VECS
NZ = 32
BX = 4
BY = 128
HALF = 8
MESH = pl.DeviceIdType.MESH
f32 = jnp.float32
bf16 = jnp.bfloat16


def split(value):
    high = value.astype(bf16)
    low = (value - high.astype(f32)).astype(bf16)
    return high, low


def harmonic(centre, neighbour):
    summed = centre + neighbour
    return 2.0 * centre * neighbour / jnp.where(summed > 0, summed, 1.0)


def basis_kernel(
    sizes,
    rs, labels, flags, perm,
    v, gram,
    stage, xl, xr, yl, yr, el, eh, kown, kxl, kxr, kyl, kyr, ct, cb, ar_y, ar_z, ar_x,
    load_sem, ksend, krecv, xsend, xrecv, ysend, yrecv, asend, arecv,
):
    gx_n, gy_n, zg, xg = sizes
    gx = lax.axis_index("gx")
    gy = lax.axis_index("gy")
    right = lax.rem(gx + 1, gx_n)
    left = lax.rem(gx + gx_n - 1, gx_n)
    above = lax.rem(gy + 1, gy_n)
    below = lax.rem(gy + gy_n - 1, gy_n)
    zi = lax.rem(gx, zg)
    xi = lax.div(gx, zg)

    def z_peer(k):
        return (xi * zg + lax.rem(zi + k, zg), gy)

    def x_peer(k):
        return (lax.rem(xi + k, xg) * zg + zi, gy)

    def y_peer(k):
        return (gx, lax.rem(gy + k, gy_n))

    peers = [(right, gy), (left, gy)]
    peers += [y_peer(k) for k in range(1, gy_n)]
    peers += [z_peer(k) for k in range(1, zg)]
    peers += [x_peer(k) for k in range(1, xg)]
    barrier = pltpu.get_barrier_semaphore()
    for peer in peers:
        pl.semaphore_signal(barrier, inc=1, device_id=peer, device_id_type=MESH)

    loads = [
        pltpu.make_async_copy(rs.at[pl.ds(c * HALF * NZ * BX, HALF * NZ * BX), :],
                              stage.at[pl.ds(c * HALF * NZ * BX, HALF * NZ * BX), :], load_sem.at[c])
        for c in range(2)
    ]
    for load in loads:
        load.start()

    for x in range(BX):
        label = labels[pl.ds(x, NZ, stride=BX), :]
        value = jnp.zeros((NZ, BY), f32)
        for region in range(perm.shape[0]):
            value = jnp.where(label == region, perm[region], value)
        kown[x] = value

    def remote(src, dst, send, recv, peer):
        return pltpu.make_async_remote_copy(
            src_ref=src, dst_ref=dst, send_sem=send, recv_sem=recv, device_id=peer, device_id_type=MESH
        )

    kcopies = [
        remote(kown.at[BX - 1], kxl, ksend.at[0], krecv.at[0], (right, gy)),
        remote(kown.at[0], kxr, ksend.at[1], krecv.at[1], (left, gy)),
        remote(kown, kyl, ksend.at[2], krecv.at[2], (gx, above)),
        remote(kown, kyr, ksend.at[3], krecv.at[3], (gx, below)),
    ]

    def xcopies(j, c):
        plane = pl.ds(j * RHS + c * HALF, HALF)
        return [
            remote(v.at[:, BX - 1, plane, :], xl.at[j, c], xsend.at[j, c, 0], xrecv.at[j, c, 0], (right, gy)),
            remote(v.at[:, 0, plane, :], xr.at[j, c], xsend.at[j, c, 1], xrecv.at[j, c, 1], (left, gy)),
        ]

    def ycopies(j, c):
        return [
            remote(eh.at[j, c], yl.at[j, c], ysend.at[j, c, 0], yrecv.at[j, c, 0], (gx, above)),
            remote(el.at[j, c], yr.at[j, c], ysend.at[j, c, 1], yrecv.at[j, c, 1], (gx, below)),
        ]

    lane = lax.broadcasted_iota(jnp.int32, (HALF, BY), 1)
    blank = jnp.zeros((HALF, BY), f32)

    def pack(value, r, low, high):
        low = jnp.where(lane == r, pltpu.roll(value, r, 1), low)
        high = jnp.where(lane == r, pltpu.roll(value, lax.rem(r + 1, BY), 1), high)
        return low, high

    pl.semaphore_wait(barrier, len(peers))
    for copy in kcopies:
        copy.start()

    for c in range(2):
        loads[c].wait()

        def relayout(z, carry, c=c):
            low, high = carry
            for x in range(BX):
                r = z * BX + x
                value = stage[pl.ds(c * HALF * NZ * BX + r, HALF, stride=NZ * BX), :]
                v[z, x, pl.ds(c * HALF, HALF), :] = value
                low, high = pack(value, r, low, high)
            return low, high

        low, high = lax.fori_loop(0, NZ, relayout, (blank, blank))
        for copy in xcopies(0, c):
            copy.start()
        el[0, c] = low
        eh[0, c] = high
        for copy in ycopies(0, c):
            copy.start()

    for copy in kcopies:
        copy.wait_recv()
    wide_lane = lax.broadcasted_iota(jnp.int32, (NZ, BY), 1)
    level = lax.broadcasted_iota(jnp.int32, (NZ, BY), 0)
    for x in range(BX):
        centre = kown[x]
        xm = kown[x - 1] if x > 0 else jnp.where(gx == 0, 0.0, kxl[...])
        xp = kown[x + 1] if x < BX - 1 else jnp.where(gx == gx_n - 1, 0.0, kxr[...])
        from_below = jnp.where(gy == 0, 0.0, kyl[x])
        from_above = jnp.where(gy == gy_n - 1, 0.0, kyr[x])
        ym = jnp.where(wide_lane == 0, pltpu.roll(from_below, 1, 1), pltpu.roll(centre, 1, 1))
        yp = jnp.where(wide_lane == BY - 1, pltpu.roll(from_above, BY - 1, 1), pltpu.roll(centre, BY - 1, 1))
        zm = jnp.where(level == 0, 0.0, pltpu.roll(centre, 1, 0))
        zp = jnp.where(level == NZ - 1, 0.0, pltpu.roll(centre, NZ - 1, 0))
        t = [harmonic(centre, other) for other in (xm, xp, ym, yp, zm, zp)]
        bottom = flags[pl.ds(x, 1), :].astype(f32)
        top = flags[pl.ds(BX + x, 1), :].astype(f32)
        boundary = jnp.where(level == 0, 2.0 * centre * bottom, 0.0)
        boundary = boundary + jnp.where(level == NZ - 1, 2.0 * centre * top, 0.0)
        diagonal = t[0] + t[1] + t[2] + t[3] + t[4] + t[5] + boundary
        divisor = jnp.where(diagonal > 0, diagonal, 1.0)
        for n in range(6):
            ct[n, x] = -(t[n] / divisor)

    def spread(block, carry):
        for n in range(6):
            for x in range(BX):
                rows = ct[n, x, pl.ds(pl.multiple_of(block * 8, 8), 8), :]
                for s in range(8):
                    cb[block * 8 + s, x, n] = jnp.broadcast_to(rows[s : s + 1, :], (HALF, BY))
        return carry

    lax.fori_loop(0, NZ // 8, spread, 0)

    for j in range(S):
        for c in range(2):
            for copy in xcopies(j, c) + ycopies(j, c):
                copy.wait_recv()
            ylow = yl[j, c]
            yhigh = yr[j, c]
            here = pl.ds(j * RHS + c * HALF, HALF)
            before = pl.ds((j - 1) * RHS + c * HALF, HALF)
            after = pl.ds((j + 1) * RHS + c * HALF, HALF)

            def advance(z, carry, j=j, c=c, ylow=ylow, yhigh=yhigh, here=here, before=before, after=after):
                low, high = carry
                zm = lax.rem(z + NZ - 1, NZ)
                zp = lax.rem(z + 1, NZ)
                row = [xl[j, c, z]] + [v[z, x, here, :] for x in range(BX)] + [xr[j, c, z]]
                for x in range(BX):
                    r = z * BX + x
                    centre = row[x + 1]
                    ym = jnp.where(lane == 0, pltpu.roll(ylow, lax.rem(BY - r, BY), 1), pltpu.roll(centre, 1, 1))
                    yp = jnp.where(lane == BY - 1, pltpu.roll(yhigh, BY - 1 - r, 1), pltpu.roll(centre, BY - 1, 1))
                    summed = (
                        cb[z, x, 0] * row[x]
                        + cb[z, x, 1] * row[x + 2]
                        + cb[z, x, 2] * ym
                        + cb[z, x, 3] * yp
                        + cb[z, x, 4] * v[zm, x, here, :]
                        + cb[z, x, 5] * v[zp, x, here, :]
                    )
                    value = summed if j == 0 else 2.0 * summed - v[z, x, before, :]
                    v[z, x, after, :] = value
                    if j < S - 1:
                        low, high = pack(value, r, low, high)
                return low, high

            low, high = lax.fori_loop(0, NZ, advance, (blank, blank))
            if j < S - 1:
                for copy in xcopies(j + 1, c):
                    copy.start()
                el[j + 1, c] = low
                eh[j + 1, c] = high
                for copy in ycopies(j + 1, c):
                    copy.start()

    def products(z, acc):
        for h in range(2):
            both = jnp.concatenate([v[z, 2 * h], v[z, 2 * h + 1]], axis=1)
            high, low = split(both)
            acc = acc + lax.dot_general(
                high, jnp.concatenate([high, low], axis=0), (((1,), (1,)), ((), ())), preferred_element_type=f32
            )
        return acc

    acc = lax.fori_loop(0, NZ, products, jnp.zeros((COLS, 2 * COLS), f32))
    cross = jnp.concatenate([acc[:, COLS:], jnp.zeros((COLS, 128 - COLS), f32)], axis=1)
    cross = jnp.concatenate([cross, jnp.zeros((128 - COLS, 128), f32)], axis=0)
    main = jnp.concatenate([acc[:, :COLS], jnp.zeros((COLS, 128 - COLS), f32)], axis=1)
    total = main + cross[:COLS] + cross.T[:COLS]

    waits = []
    for phase, (buffer, index, count, peer_of) in enumerate(
        [(ar_y, gy, gy_n, y_peer), (ar_z, zi, zg, z_peer), (ar_x, xi, xg, x_peer)]
    ):
        buffer[index] = total
        copies = [
            remote(buffer.at[index], buffer.at[index], asend.at[phase, k - 1], arecv.at[phase, k - 1], peer_of(k))
            for k in range(1, count)
        ]
        for copy in copies:
            copy.start()
        for copy in copies:
            copy.wait_recv()
        waits += copies
        total = buffer[0]
        for k in range(1, count):
            total = total + buffer[k]
    gram[...] = total

    for copy in kcopies + waits:
        copy.wait_send()
    for j in range(S):
        for c in range(2):
            for copy in xcopies(j, c) + ycopies(j, c):
                copy.wait_send()


def factor(gram):
    count = COLS // 8
    lane = lax.broadcasted_iota(jnp.int32, (8, 128), 1)
    row = lax.broadcasted_iota(jnp.int32, (8, 128), 0)
    left = [gram[8 * b : 8 * b + 8, :] for b in range(count)]
    right = [jnp.where(lane == row + 8 * b, 1.0, 0.0).astype(f32) for b in range(count)]
    for k in range(COLS):
        b, s = divmod(k, 8)
        pivot_left = left[b][s : s + 1, :]
        pivot_right = right[b][s : s + 1, :]
        inverse = 1.0 / pivot_left[:, k : k + 1]
        scaled_left = pivot_left * inverse
        scaled_right = pivot_right * inverse
        for i in range(b, count):
            column = left[i][:, k : k + 1]
            if i == b:
                column = jnp.where(row[:, :1] > s, column, 0.0)
            left[i] = left[i] - column * scaled_left
            right[i] = right[i] - column * scaled_right
    for b in range(count):
        diagonal = jnp.sum(jnp.where(lane == row + 8 * b, left[b], 0.0), axis=1, keepdims=True)
        scale = 1.0 / jnp.sqrt(diagonal)
        left[b] = jnp.where(lane >= row + 8 * b, left[b], 0.0) * scale
        right[b] = right[b] * scale
    return jnp.concatenate(left, axis=0), jnp.concatenate(right, axis=0)


def finish_kernel(cells, v, gram, out, r_out, stage, sems):
    upper, inverse = factor(gram[...] / cells)
    r_out[...] = upper[:, :COLS]
    high = inverse.astype(bf16).astype(f32)
    low = inverse - high
    wide_high = jnp.concatenate([high, jnp.zeros((COLS, 128), f32)], axis=1)
    wide_low = jnp.concatenate([low, jnp.zeros((COLS, 128), f32)], axis=1)
    weights = wide_high + pltpu.roll(wide_high, COLS, 1) + pltpu.roll(wide_low, 2 * COLS, 1)
    weights = weights[:, : 3 * COLS].astype(bf16)
    groups = 4
    per = NZ // groups
    copies = []
    for group in range(groups):
        def block(z, carry):
            for h in range(2):
                both = jnp.concatenate([v[z, 2 * h], v[z, 2 * h + 1]], axis=1)
                vh, vl = split(both)
                q = jnp.dot(weights, jnp.concatenate([vh, vl, vh], axis=0), preferred_element_type=f32)
                r = z * BX + 2 * h
                stage[pl.ds(r, COLS, stride=NZ * BX), :] = q[:, :BY]
                stage[pl.ds(r + 1, COLS, stride=NZ * BX), :] = q[:, BY:]
            return carry

        lax.fori_loop(group * per, (group + 1) * per, block, 0)
        rows = pl.ds(group * per * BX, per * BX)
        copy = pltpu.make_async_copy(
            stage.reshape(COLS, NZ * BX, BY).at[:, rows, :], out.at[:, rows, :], sems.at[group]
        )
        copy.start()
        copies.append(copy)
    for copy in copies:
        copy.wait()


def per_device(sizes, cells, right_sides, region_labels, face_flags, region_perm):
    gx_n, gy_n, zg, xg = sizes
    vmem = pl.BlockSpec(memory_space=pltpu.VMEM)
    hbm = pl.BlockSpec(memory_space=pl.ANY)
    v, gram = pl.pallas_call(
        functools.partial(basis_kernel, sizes),
        out_shape=(pltpu.VMEM((NZ, BX, COLS, BY), f32), pltpu.VMEM((COLS, 128), f32)),
        in_specs=[hbm, vmem, vmem, pl.BlockSpec(memory_space=pltpu.SMEM)],
        out_specs=(vmem, vmem),
        scratch_shapes=[
            pltpu.VMEM((RHS * NZ * BX, BY), f32),
            pltpu.VMEM((S, 2, NZ, HALF, BY), f32),
            pltpu.VMEM((S, 2, NZ, HALF, BY), f32),
            pltpu.VMEM((S, 2, HALF, BY), f32),
            pltpu.VMEM((S, 2, HALF, BY), f32),
            pltpu.VMEM((S, 2, HALF, BY), f32),
            pltpu.VMEM((S, 2, HALF, BY), f32),
            pltpu.VMEM((BX, NZ, BY), f32),
            pltpu.VMEM((NZ, BY), f32),
            pltpu.VMEM((NZ, BY), f32),
            pltpu.VMEM((BX, NZ, BY), f32),
            pltpu.VMEM((BX, NZ, BY), f32),
            pltpu.VMEM((6, BX, NZ, BY), f32),
            pltpu.VMEM((NZ, BX, 6, HALF, BY), f32),
            pltpu.VMEM((gy_n, COLS, 128), f32),
            pltpu.VMEM((zg, COLS, 128), f32),
            pltpu.VMEM((xg, COLS, 128), f32),
            pltpu.SemaphoreType.DMA((2,)),
            pltpu.SemaphoreType.DMA((4,)),
            pltpu.SemaphoreType.DMA((4,)),
            pltpu.SemaphoreType.DMA((S, 2, 2)),
            pltpu.SemaphoreType.DMA((S, 2, 2)),
            pltpu.SemaphoreType.DMA((S, 2, 2)),
            pltpu.SemaphoreType.DMA((S, 2, 2)),
            pltpu.SemaphoreType.DMA((3, 8)),
            pltpu.SemaphoreType.DMA((3, 8)),
        ],
        compiler_params=pltpu.CompilerParams(
            collective_id=0, has_side_effects=True, vmem_limit_bytes=40 * 1024 * 1024
        ),
        name="basis",
    )(
        right_sides.reshape(RHS * NZ * BX, BY),
        region_labels.reshape(NZ * BX, BY),
        face_flags.reshape(2 * BX, BY),
        region_perm,
    )
    out, upper = pl.pallas_call(
        functools.partial(finish_kernel, cells),
        out_shape=(
            jax.ShapeDtypeStruct((COLS, NZ * BX, BY), f32),
            jax.ShapeDtypeStruct((COLS, COLS), f32),
        ),
        in_specs=[vmem, vmem],
        out_specs=(hbm, vmem),
        scratch_shapes=[pltpu.VMEM((COLS * NZ * BX, BY), f32), pltpu.SemaphoreType.DMA((4,))],
        compiler_params=pltpu.CompilerParams(vmem_limit_bytes=40 * 1024 * 1024),
        name="finish",
    )(v, gram)
    return out.reshape(COLS, NZ, BX, BY), upper


def solution(mesh):
    gx_n, gy_n = mesh.shape["gx"], mesh.shape["gy"]
    zg = 8 if gx_n % 8 == 0 else 2
    sizes = (gx_n, gy_n, zg, gx_n // zg)
    cells = NZ * BX * BY * gx_n * gy_n
    placed = (P(None, None, "gx", "gy"), P(None, "gx", "gy"), P(None, "gx", "gy"), P())
    return jax.shard_map(
        functools.partial(per_device, sizes, cells),
        mesh=mesh,
        in_specs=placed,
        out_specs=(P(None, None, "gx", "gy"), P()),
        check_vma=False,
    )
```

profile of v0, /device:TPU:1, one launch (start us, length us, event | category | flops | bytes accessed | tf_op | source)
XLA Modules:
  0.0 103.9 jit_solution(18200431850064156485)
XLA Ops:
  0.6 0.0 copy-start
  0.6 1.2 %copy-done = f32[16,32,4,128]{3,2,1,0:T(4,128)S(1)} copy-done((f32[16,32,4,128]{3,2,1,0:T(4,128)S(1)}, f32[16,32,4,128]{3,2,1,0:T(4,128)}, u32[]{:S(2)}) %copy-start) | copy-done | bytes 1048600
  1.9 0.0 copy-start.1
  1.9 0.8 copy-done.1
  2.7 0.0 copy-start.2
  2.7 0.7 copy-done.2
  3.4 0.0 copy-start.3
  3.4 0.7 copy-done.3
  4.0 83.5 %basis.1 = (f32[32,4,80,128]{3,2,1,0:T(8,128)S(1)}, f32[80,128]{1,0:T(8,128)S(1)}) custom-call(f32[2048,128]{1,0:T(8,128)S(1)} %bitcast.4, s32[128,128]{1,0:T(8,128)S(1)} %bitcast.5, s32[8,128]{1,0:T(8,128)S(1)} %bitcast.6, f32[8]{0:T(128)S(1)} %copy-done.3), custom_call_target="tpu_custom_call" | custom-call | tf_op jit(solution)/shard_map/basis/pallas_call | solution.py:323
  87.5 16.4 %finish.1 = (f32[80,128,128]{2,1,0:T(8,128)}, f32[80,80]{1,0:T(8,128)}) custom-call(f32[32,4,80,128]{3,2,1,0:T(8,128)S(1)} %get-tuple-element.6.v, f32[80,128]{1,0:T(8,128)S(1)} %get-tuple-element.7.gram), custom_call_target="tpu_custom_call" | custom-call | tf_op jit(solution)/shard_map/finish/pallas_call | solution.py:366
Async XLA Ops:
  0.6 1.2 %copy-start = (f32[16,32,4,128]{3,2,1,0:T(4,128)S(1)}, f32[16,32,4,128]{3,2,1,0:T(4,128)}, u32[]{:S(2)}) copy-start(f32[16,32,4,128]{3,2,1,0:T(4,128)} %param.4) | copy-start | bytes 3145732
  1.9 0.8 copy-start.1
  2.7 0.7 copy-start.2
  3.4 0.7 copy-start.3
where the time goes:
time: 106 us; the launch traced here: 104 us
  Pallas kernels  99.9 us (94%)
  local copies, waits for them, and re-layouts  3.4 us (3%)
    pallas_call x1, Pallas kernels, per_device(): pl.pallas_call(functools.partial(basis_kernel, sizes), out_shape=(pltpu.V...  83.5 us
    pallas_call x1, Pallas kernels, per_device(): pl.pallas_call(functools.partial(finish_kernel, cells), out_shape=(jax.Sh...  16.4 us
    unnamed x8, local copies, waits for them, and re-layouts  3.4 us

commit v1 on v0

v1 whole, which is shorter than its diff:
```python
import functools
import jax
import jax.numpy as jnp
from jax import lax
from jax.experimental import pallas as pl
from jax.experimental.pallas import tpu as pltpu
from jax.sharding import PartitionSpec as P

RHS = 16
S = 4
VECS = S + 1
COLS = RHS * VECS
NZ = 32
BX = 4
BY = 128
HALF = 8
LEAD = RHS * S
LEVELS = 8
CHUNKS = NZ // LEVELS
ROWS = LEVELS * BX
NT = (((1,), (1,)), ((), ()))
NN = (((1,), (0,)), ((), ()))
MESH = pl.DeviceIdType.MESH
f32 = jnp.float32
bf16 = jnp.bfloat16


def split(value):
    high = value.astype(bf16)
    low = (value - high.astype(f32)).astype(bf16)
    return high, low


def harmonic(centre, neighbour):
    summed = centre + neighbour
    return 2.0 * centre * neighbour / jnp.where(summed > 0, summed, 1.0)


def basis_kernel(
    sizes, cells,
    rs, labels_hbm, flags_hbm, perm,
    v, last_gram, lead,
    stage, labels, flags, xl, xr, edge, yl, yr, kown, kxl, kxr, kyl, kyr, ct, cb,
    acc_lead, acc_last, lead_own, lead_y, lead_z, lead_x, lead_all, last_y, last_z, last_x,
    load_sem, ksend, krecv, xsend, xrecv, ysend, yrecv, asend, arecv,
):
    gx_n, gy_n, zg, xg = sizes
    gx = lax.axis_index("gx")
    gy = lax.axis_index("gy")
    right = lax.rem(gx + 1, gx_n)
    left = lax.rem(gx + gx_n - 1, gx_n)
    above = lax.rem(gy + 1, gy_n)
    below = lax.rem(gy + gy_n - 1, gy_n)
    zi = lax.rem(gx, zg)
    xi = lax.div(gx, zg)

    def z_peer(k):
        return (xi * zg + lax.rem(zi + k, zg), gy)

    def x_peer(k):
        return (lax.rem(xi + k, xg) * zg + zi, gy)

    def y_peer(k):
        return (gx, lax.rem(gy + k, gy_n))

    loads = [
        pltpu.make_async_copy(labels_hbm, labels, load_sem.at[CHUNKS]),
        pltpu.make_async_copy(flags_hbm, flags, load_sem.at[CHUNKS + 1]),
    ] + [
        pltpu.make_async_copy(
            rs.at[:, pl.ds(q * ROWS, ROWS), :], stage.reshape(CHUNKS, RHS, ROWS, BY).at[q], load_sem.at[q]
        )
        for q in range(CHUNKS)
    ]
    for load in loads:
        load.start()
    peers = [(right, gy), (left, gy)]
    peers += [y_peer(k) for k in range(1, gy_n)]
    peers += [z_peer(k) for k in range(1, zg)]
    peers += [x_peer(k) for k in range(1, xg)]
    barrier = pltpu.get_barrier_semaphore()
    for peer in peers:
        pl.semaphore_signal(barrier, inc=1, device_id=peer, device_id_type=MESH)

    loads[0].wait()
    loads[1].wait()
    for x in range(BX):
        label = labels[pl.ds(x, NZ, stride=BX), :]
        value = jnp.zeros((NZ, BY), f32)
        for region in range(perm.shape[0]):
            value = jnp.where(label == region, perm[region], value)
        kown[x] = value

    def remote(src, dst, send, recv, peer):
        return pltpu.make_async_remote_copy(
            src_ref=src, dst_ref=dst, send_sem=send, recv_sem=recv, device_id=peer, device_id_type=MESH
        )

    kcopies = [
        remote(kown.at[BX - 1], kxl, ksend.at[0], krecv.at[0], (right, gy)),
        remote(kown.at[0], kxr, ksend.at[1], krecv.at[1], (left, gy)),
        remote(kown, kyl, ksend.at[2], krecv.at[2], (gx, above)),
        remote(kown, kyr, ksend.at[3], krecv.at[3], (gx, below)),
    ]

    def copies_of(j, q):
        levels = pl.ds(q * LEVELS, LEVELS)
        plane = pl.ds(j * RHS, RHS)
        return [
            remote(v.at[levels, BX - 1, plane, :], xl.at[j, q], xsend.at[j, q, 0], xrecv.at[j, q, 0], (right, gy)),
            remote(v.at[levels, 0, plane, :], xr.at[j, q], xsend.at[j, q, 1], xrecv.at[j, q, 1], (left, gy)),
            remote(edge.at[j, q], yl.at[j, q], ysend.at[j, q, 0], yrecv.at[j, q, 0], (gx, above)),
            remote(edge.at[j, q], yr.at[j, q], ysend.at[j, q, 1], yrecv.at[j, q, 1], (gx, below)),
        ]

    lane = lax.broadcasted_iota(jnp.int32, (HALF, BY), 1)
    pair = lax.div(lane, 2)
    odd = lax.rem(lane, 2) == 1

    def pack(value, rr, packed):
        return jnp.where(pair == rr, pltpu.roll(value, 2 * rr + 1, 1), packed)

    pl.semaphore_wait(barrier, len(peers))
    for copy in kcopies:
        copy.start()
    for q in range(CHUNKS):
        loads[2 + q].wait()

    def relayout(q, carry):
        packed = [jnp.zeros((HALF, BY), f32) for _ in range(2)]
        for s in range(LEVELS):
            for x in range(BX):
                rr = s * BX + x
                value = stage[pl.ds(q * RHS * ROWS + rr, RHS, stride=ROWS), :]
                v[q * LEVELS + s, x, :RHS, :] = value
                for h in range(2):
                    packed[h] = pack(value[h * HALF : (h + 1) * HALF], rr, packed[h])
        for h in range(2):
            edge[0, q, h] = packed[h]
        for copy in copies_of(0, q):
            copy.start()
        return carry

    lax.fori_loop(0, CHUNKS, relayout, 0)

    for copy in kcopies:
        copy.wait_recv()
    wide_lane = lax.broadcasted_iota(jnp.int32, (NZ, BY), 1)
    level = lax.broadcasted_iota(jnp.int32, (NZ, BY), 0)
    for x in range(BX):
        centre = kown[x]
        xm = kown[x - 1] if x > 0 else jnp.where(gx == 0, 0.0, kxl[...])
        xp = kown[x + 1] if x < BX - 1 else jnp.where(gx == gx_n - 1, 0.0, kxr[...])
        from_below = jnp.where(gy == 0, 0.0, kyl[x])
        from_above = jnp.where(gy == gy_n - 1, 0.0, kyr[x])
        ym = jnp.where(wide_lane == 0, pltpu.roll(from_below, 1, 1), pltpu.roll(centre, 1, 1))
        yp = jnp.where(wide_lane == BY - 1, pltpu.roll(from_above, BY - 1, 1), pltpu.roll(centre, BY - 1, 1))
        zm = jnp.where(level == 0, 0.0, pltpu.roll(centre, 1, 0))
        zp = jnp.where(level == NZ - 1, 0.0, pltpu.roll(centre, NZ - 1, 0))
        t = [harmonic(centre, other) for other in (xm, xp, ym, yp, zm, zp)]
        bottom = flags[pl.ds(x, 1), :].astype(f32)
        top = flags[pl.ds(BX + x, 1), :].astype(f32)
        boundary = jnp.where(level == 0, 2.0 * centre * bottom, 0.0)
        boundary = boundary + jnp.where(level == NZ - 1, 2.0 * centre * top, 0.0)
        diagonal = t[0] + t[1] + t[2] + t[3] + t[4] + t[5] + boundary
        divisor = jnp.where(diagonal > 0, diagonal, 1.0)
        for n in range(6):
            ct[n, x] = -(t[n] / divisor)

    def spread(block, carry):
        for n in range(6):
            for x in range(BX):
                rows = ct[n, x, pl.ds(pl.multiple_of(block * 8, 8), 8), :]
                for s in range(8):
                    cb[block * 8 + s, x, n] = jnp.broadcast_to(rows[s : s + 1, :], (HALF, BY))
        return carry

    lax.fori_loop(0, NZ // 8, spread, 0)

    def advance(j, q):
        for copy in copies_of(j, q):
            copy.wait_recv()
        base = q * LEVELS
        merged = [
            jnp.where(odd, pltpu.roll(yl[j, q, h], 1, 1), pltpu.roll(yr[j, q, h], BY - 1, 1)) for h in range(2)
        ]
        packed = [jnp.zeros((HALF, BY), f32) for _ in range(2)]
        for s in range(LEVELS):
            z = base + s
            zm = lax.rem(z + NZ - 1, NZ) if s == 0 else z - 1
            zp = lax.rem(z + 1, NZ) if s == LEVELS - 1 else z + 1
            for x in range(BX):
                rr = s * BX + x
                coupling = [cb[z, x, n] for n in range(6)]
                for h in range(2):
                    here = pl.ds(j * RHS + h * HALF, HALF)
                    rows = pl.ds(h * HALF, HALF)
                    centre = v[z, x, here, :]
                    xm = v[z, x - 1, here, :] if x > 0 else xl[j, q, s, rows, :]
                    xp = v[z, x + 1, here, :] if x < BX - 1 else xr[j, q, s, rows, :]
                    ends = pltpu.roll(merged[h], BY - 1 - 2 * rr, 1)
                    ym = jnp.where(lane == 0, ends, pltpu.roll(centre, 1, 1))
                    yp = jnp.where(lane == BY - 1, ends, pltpu.roll(centre, BY - 1, 1))
                    summed = (
                        coupling[0] * xm
                        + coupling[1] * xp
                        + coupling[2] * ym
                        + coupling[3] * yp
                        + coupling[4] * v[zm, x, here, :]
                        + coupling[5] * v[zp, x, here, :]
                    )
                    value = summed if j == 0 else 2.0 * summed - v[z, x, pl.ds((j - 1) * RHS + h * HALF, HALF), :]
                    v[z, x, pl.ds((j + 1) * RHS + h * HALF, HALF), :] = value
                    if j < S - 1:
                        packed[h] = pack(value, rr, packed[h])
        if j < S - 1:
            for h in range(2):
                edge[j + 1, q, h] = packed[h]
            for copy in copies_of(j + 1, q):
                copy.start()

    def lead_products(q):
        total = jnp.zeros((LEAD, 2 * LEAD), f32)
        for s in range(LEVELS):
            wide = jnp.concatenate([v[q * LEVELS + s, x, :LEAD, :] for x in range(BX)], axis=1)
            high, low = split(wide)
            total = total + lax.dot_general(high, jnp.concatenate([high, low], axis=0), NT, preferred_element_type=f32)
        acc_lead[...] += total

    def last_products(q):
        total = jnp.zeros((2 * RHS, 2 * COLS), f32)
        for s in range(LEVELS):
            wide = jnp.concatenate([v[q * LEVELS + s, x] for x in range(BX)], axis=1)
            high, low = split(wide)
            total = total + lax.dot_general(
                jnp.concatenate([high[LEAD:], low[LEAD:]], axis=0),
                jnp.concatenate([high, low], axis=0),
                NT,
                preferred_element_type=f32,
            )
        acc_last[...] += total

    def exchange(phase, buffer, index, count, peer_of, source=None):
        def of(k):
            src = buffer.at[index] if source is None else source.at[lax.rem(index + k, count)]
            return remote(src, buffer.at[index], asend.at[phase, k - 1], arecv.at[phase, k - 1], peer_of(k))

        return [of(k) for k in range(1, count)]

    steps_lead = [
        exchange(0, lead_y, gy, gy_n, y_peer, lead_own),
        exchange(1, lead_z, zi, zg, z_peer),
        exchange(2, lead_x, xi, xg, x_peer),
        exchange(3, lead_all, gy, gy_n, y_peer),
    ]
    steps_last = [
        exchange(4, last_y, gy, gy_n, y_peer),
        exchange(5, last_z, zi, zg, z_peer),
        exchange(6, last_x, xi, xg, x_peer),
    ]

    def send(step):
        for copy in step:
            copy.start()

    def collect(step, buffer):
        for copy in step:
            copy.wait_recv()
        total = buffer[0]
        for k in range(1, len(step) + 1):
            total = total + buffer[k]
        return total

    acc_lead[...] = jnp.zeros_like(acc_lead)
    acc_last[...] = jnp.zeros_like(acc_last)

    def loop(j, more=None):
        def body(q, carry):
            advance(j, q)
            if more is not None:
                more(q)
            return carry

        lax.fori_loop(0, CHUNKS, body, 0)

    loop(0)
    loop(1)
    loop(2, lead_products)

    partial = acc_lead[...]
    mirrored = jnp.concatenate([partial, jnp.zeros((128 - LEAD, 128), f32)], axis=0).T[LEAD : 2 * LEAD]
    lead_lane = lax.broadcasted_iota(jnp.int32, (LEAD, 128), 1)
    partial = jnp.where(lead_lane < LEAD, partial + pltpu.roll(partial, LEAD, 1), 0.0) + mirrored
    for b in range(LEAD // 8):
        lead_own[b] = partial[8 * b : 8 * b + 8]
    lead_y[gy] = lead_own[gy]
    send(steps_lead[0])

    def beside(q):
        last_products(q)

        @pl.when(q == 0)
        def _():
            lead_z[zi] = collect(steps_lead[0], lead_y)
            send(steps_lead[1])

        @pl.when(q == 1)
        def _():
            lead_x[xi] = collect(steps_lead[1], lead_z)
            send(steps_lead[2])

        @pl.when(q == 2)
        def _():
            lead_all[gy] = collect(steps_lead[2], lead_x)
            send(steps_lead[3])

    loop(3, beside)

    partial = acc_last[...]
    last_y[gy] = jnp.concatenate(
        [partial[:RHS, :COLS] + partial[:RHS, COLS:] + partial[RHS:, :COLS], jnp.zeros((RHS, 128 - COLS), f32)], axis=1
    )
    send(steps_last[0])
    for copy in steps_lead[3]:
        copy.wait_recv()
    rows = eliminate_start([lead_all[b] * (1.0 / cells) for b in range(LEAD // 8)], LEAD)
    rows = eliminate(rows, 0, 24)
    last_z[zi] = collect(steps_last[0], last_y)
    send(steps_last[1])
    rows = eliminate(rows, 24, 48)
    last_x[xi] = collect(steps_last[1], last_z)
    send(steps_last[2])
    rows = eliminate(rows, 48, LEAD)
    lead[...] = jnp.concatenate(eliminate_end(rows, LEAD), axis=0)
    last_gram[...] = collect(steps_last[2], last_x) * (1.0 / cells)

    for copy in kcopies:
        copy.wait_send()

    def drain(q, carry):
        for j in range(S):
            for copy in copies_of(j, q):
                copy.wait_send()
        return carry

    lax.fori_loop(0, CHUNKS, drain, 0)
    for step in steps_lead + steps_last:
        for copy in step:
            copy.wait_send()


def eliminate_start(blocks, size):
    lane = lax.broadcasted_iota(jnp.int32, (8, 128), 1)
    row = lax.broadcasted_iota(jnp.int32, (8, 128), 0)
    return [
        jnp.where(lane < size, block, jnp.where(lane - size == row + 8 * b, 1.0, 0.0).astype(f32))
        for b, block in enumerate(blocks)
    ]


def eliminate(rows, begin, end):
    rows = list(rows)
    sub = lax.broadcasted_iota(jnp.int32, (8, 1), 0)
    for k in range(begin, end):
        b, s = divmod(k, 8)
        pivot = rows[b][s : s + 1, :]
        scaled = pivot * (1.0 / pivot[:, k : k + 1])
        for i in range(b, len(rows)):
            column = rows[i][:, k : k + 1]
            if i == b:
                column = jnp.where(sub > s, column, 0.0)
            rows[i] = rows[i] - column * scaled
    return rows


def eliminate_end(rows, size):
    lane = lax.broadcasted_iota(jnp.int32, (8, 128), 1)
    row = lax.broadcasted_iota(jnp.int32, (8, 128), 0)
    done = []
    for b, block in enumerate(rows):
        diagonal = jnp.sum(jnp.where(lane == row + 8 * b, block, 0.0), axis=1, keepdims=True)
        block = jnp.where((lane >= row + 8 * b) & (lane - size <= row + 8 * b), block, 0.0)
        done.append(block / jnp.sqrt(diagonal))
    return done


def exact(a, b, dims):
    return lax.dot_general(a, b, dims, precision=lax.Precision.HIGHEST, preferred_element_type=f32)


def finish_kernel(v, last_gram, lead, out, r_out, stage, sems):
    upper = lead[:, :LEAD]
    inverse = lead[:, LEAD:]
    against = last_gram[:, :LEAD]
    cross = exact(against, inverse, NT)
    schur = last_gram[:, LEAD:COLS] - exact(cross, cross, NT)
    back = exact(cross, inverse, NN)
    padded = jnp.concatenate([schur, jnp.zeros((RHS, 128 - RHS), f32)], axis=1)
    rows = eliminate_start([padded[:8], padded[8:]], RHS)
    rows = eliminate_end(eliminate(rows, 0, RHS), RHS)
    corner = jnp.concatenate(rows, axis=0)
    corner_upper = corner[:, :RHS]
    corner_inverse = corner[:, RHS : 2 * RHS]
    back = -exact(corner_inverse, back, NN)

    tall = jnp.concatenate([cross, jnp.zeros((RHS, 128 - LEAD), f32)], axis=1)
    tall = jnp.concatenate([tall, jnp.zeros((128 - RHS, 128), f32)], axis=0).T[:LEAD, :RHS]
    r_out[...] = jnp.concatenate(
        [
            jnp.concatenate([upper, tall], axis=1),
            jnp.concatenate([jnp.zeros((RHS, LEAD), f32), corner_upper], axis=1),
        ],
        axis=0,
    )
    whole = jnp.concatenate(
        [
            jnp.concatenate([inverse, jnp.zeros((LEAD, 256 - LEAD), f32)], axis=1),
            jnp.concatenate([back, corner_inverse, jnp.zeros((RHS, 256 - COLS), f32)], axis=1),
        ],
        axis=0,
    )
    high = whole.astype(bf16).astype(f32)
    low = whole - high
    weights = high + pltpu.roll(high, COLS, 1) + pltpu.roll(low, 2 * COLS, 1)
    weights = weights[:, : 3 * COLS].astype(bf16)
    groups = 4
    per = NZ // groups
    copies = []
    for group in range(groups):
        def block(step, carry):
            for s in range(4):
                z = step * 4 + s
                for h in range(2):
                    both = jnp.concatenate([v[z, 2 * h], v[z, 2 * h + 1]], axis=1)
                    vh, vl = split(both)
                    q = jnp.dot(weights, jnp.concatenate([vh, vl, vh], axis=0), preferred_element_type=f32)
                    r = z * BX + 2 * h
                    stage[pl.ds(r, COLS, stride=NZ * BX), :] = q[:, :BY]
                    stage[pl.ds(r + 1, COLS, stride=NZ * BX), :] = q[:, BY:]
            return carry

        lax.fori_loop(group * per // 4, (group + 1) * per // 4, block, 0)
        rows = pl.ds(group * per * BX, per * BX)
        copy = pltpu.make_async_copy(
            stage.reshape(COLS, NZ * BX, BY).at[:, rows, :], out.at[:, rows, :], sems.at[group]
        )
        copy.start()
        copies.append(copy)
    for copy in copies:
        copy.wait()


def per_device(sizes, cells, right_sides, region_labels, face_flags, region_perm):
    gx_n, gy_n, zg, xg = sizes
    vmem = pl.BlockSpec(memory_space=pltpu.VMEM)
    hbm = pl.BlockSpec(memory_space=pltpu.HBM)
    scratch = [
        (CHUNKS * RHS * ROWS, BY),
        (NZ * BX, BY, jnp.int32),
        (2 * BX, BY, jnp.int32),
        (S, CHUNKS, LEVELS, RHS, BY),
        (S, CHUNKS, LEVELS, RHS, BY),
        (S, CHUNKS, 2, HALF, BY),
        (S, CHUNKS, 2, HALF, BY),
        (S, CHUNKS, 2, HALF, BY),
        (BX, NZ, BY),
        (NZ, BY),
        (NZ, BY),
        (BX, NZ, BY),
        (BX, NZ, BY),
        (6, BX, NZ, BY),
        (NZ, BX, 6, HALF, BY),
        (LEAD, 2 * LEAD),
        (2 * RHS, 2 * COLS),
        (LEAD // 8, 8, 128),
        (gy_n, 8, 128),
        (zg, 8, 128),
        (xg, 8, 128),
        (LEAD // 8, 8, 128),
        (gy_n, RHS, 128),
        (zg, RHS, 128),
        (xg, RHS, 128),
    ]
    scratch = [
        pltpu.VMEM(shape[:-1], shape[-1]) if shape[-1] is jnp.int32 else pltpu.VMEM(shape, f32) for shape in scratch
    ]
    dma = pltpu.SemaphoreType.DMA
    scratch += [dma((CHUNKS + 2,)), dma((4,)), dma((4,))]
    scratch += [dma((S, CHUNKS, 2)) for _ in range(4)] + [dma((7, 8)), dma((7, 8))]
    v, last_gram, lead = pl.pallas_call(
        functools.partial(basis_kernel, sizes, cells),
        out_shape=(
            pltpu.VMEM((NZ, BX, COLS, BY), f32),
            pltpu.VMEM((RHS, 128), f32),
            pltpu.VMEM((LEAD, 2 * LEAD), f32),
        ),
        in_specs=[hbm, hbm, hbm, pl.BlockSpec(memory_space=pltpu.SMEM)],
        out_specs=(vmem, vmem, vmem),
        scratch_shapes=scratch,
        compiler_params=pltpu.CompilerParams(
            collective_id=0, has_side_effects=True, vmem_limit_bytes=40 * 1024 * 1024
        ),
        name="basis",
    )(
        *(pltpu.with_memory_space_constraint(a, pltpu.HBM) for a in (
            right_sides.reshape(RHS, NZ * BX, BY),
            region_labels.reshape(NZ * BX, BY),
            face_flags.reshape(2 * BX, BY),
            region_perm,
        )),
    )
    out, upper = pl.pallas_call(
        finish_kernel,
        out_shape=(
            jax.ShapeDtypeStruct((COLS, NZ * BX, BY), f32),
            jax.ShapeDtypeStruct((COLS, COLS), f32),
        ),
        in_specs=[vmem, vmem, vmem],
        out_specs=(hbm, vmem),
        scratch_shapes=[pltpu.VMEM((COLS * NZ * BX, BY), f32), dma((4,))],
        compiler_params=pltpu.CompilerParams(vmem_limit_bytes=40 * 1024 * 1024),
        name="finish",
    )(v, last_gram, lead)
    return out.reshape(COLS, NZ, BX, BY), upper


def solution(mesh):
    gx_n, gy_n = mesh.shape["gx"], mesh.shape["gy"]
    zg = 8 if gx_n % 8 == 0 else 2
    sizes = (gx_n, gy_n, zg, gx_n // zg)
    cells = NZ * BX * BY * gx_n * gy_n
    placed = (P(None, None, "gx", "gy"), P(None, "gx", "gy"), P(None, "gx", "gy"), P())
    return jax.shard_map(
        functools.partial(per_device, sizes, cells),
        mesh=mesh,
        in_specs=placed,
        out_specs=(P(None, None, "gx", "gy"), P()),
        check_vma=False,
    )
```

time: 106 us -> 72.5 us (0.68); the launches traced: 104 us -> 72.4 us
  Pallas kernels: 99.9 us -> 71.8 us
  local copies, waits for them, and re-layouts: 3.4 us -> 0 us
    pallas_call x2, Pallas kernels: 99.9 us -> 71.8 us  [the longest x1 63.1 us: per_device(): pl.pallas_call(functools.partial(basis_kernel, sizes, cells), out_shape=(...]
    unnamed x8 -> x0, local copies, waits for them, and re-layouts: 3.4 us -> none
where the time goes in v1:
time: 72.5 us; the launch traced here: 72.4 us
  Pallas kernels  71.8 us (99%)
    pallas_call x1, Pallas kernels, per_device(): pl.pallas_call(functools.partial(basis_kernel, sizes, cells), out_shape=(...  63.1 us
    pallas_call x1, Pallas kernels, per_device(): pl.pallas_call(finish_kernel, out_shape=(jax.ShapeDtypeStruct((COLS, NZ *...  8.66 us

profile of v1, /device:TPU:1, one launch (start us, length us, event | category | flops | bytes accessed | tf_op | source)
XLA Modules:
  0.0 72.4 jit_solution(6162926136121647472)
XLA Ops:
  0.6 63.1 %basis.1 = (f32[32,4,80,128]{3,2,1,0:T(8,128)S(1)}, f32[16,128]{1,0:T(8,128)S(1)}, f32[64,128]{1,0:T(8,128)S(1)}) custom-call(f32[16,128,128]{2,1,0:T(8,128)} %bitcast.4, s32[128,128]{1,0:T(8,128)} %bitcast.5, s32[8,128]{1,0:T(8,128)} %bitcast.6, f32[8]{0:T(128)} %perm.1), custom_call_target="tpu_custom_call" | custom-call | tf_op jit(solution)/shard_map/basis/pallas_call | solution.py:490
  63.7 8.7 %finish.1 = (f32[80,128,128]{2,1,0:T(8,128)}, f32[80,80]{1,0:T(8,128)}) custom-call(f32[32,4,80,128]{3,2,1,0:T(8,128)S(1)} %get-tuple-element.7.v, f32[16,128]{1,0:T(8,128)S(1)} %get-tuple-element.8.last_gram, f32[64,128]{1,0:T(8,128)S(1)} %get-tuple-element.9.lead), custom_call_target="tpu_custom_call" | custom-call | tf_op jit(solution)/shard_map/finish/pallas_call | solution.py:512

commit v2 on v1

--- a/solution.py
+++ b/solution.py
@@ -18,6 +18,7 @@
 LEVELS = 8
 CHUNKS = NZ // LEVELS
 ROWS = LEVELS * BX
+PITCH = NZ * BX + 8
 NT = (((1,), (1,)), ((), ()))
 NN = (((1,), (0,)), ((), ()))
 MESH = pl.DeviceIdType.MESH
@@ -41,7 +42,7 @@
     rs, labels_hbm, flags_hbm, perm,
     v, last_gram, lead,
     stage, labels, flags, xl, xr, edge, yl, yr, kown, kxl, kxr, kyl, kyr, ct, cb,
-    acc_lead, acc_last, lead_own, lead_y, lead_z, lead_x, lead_all, last_y, last_z, last_x,
+    acc_lead, acc_last, lead_y, lead_z, lead_x, last_y, last_z, last_x,
     load_sem, ksend, krecv, xsend, xrecv, ysend, yrecv, asend, arecv,
 ):
     gx_n, gy_n, zg, xg = sizes
@@ -120,9 +121,6 @@
     def pack(value, rr, packed):
         return jnp.where(pair == rr, pltpu.roll(value, 2 * rr + 1, 1), packed)
 
-    pl.semaphore_wait(barrier, len(peers))
-    for copy in kcopies:
-        copy.start()
     for q in range(CHUNKS):
         loads[2 + q].wait()
 
@@ -137,11 +135,18 @@
                     packed[h] = pack(value[h * HALF : (h + 1) * HALF], rr, packed[h])
         for h in range(2):
             edge[0, q, h] = packed[h]
+        return carry
+
+    def first(q, carry):
         for copy in copies_of(0, q):
             copy.start()
         return carry
 
     lax.fori_loop(0, CHUNKS, relayout, 0)
+    pl.semaphore_wait(barrier, len(peers))
+    for copy in kcopies:
+        copy.start()
+    lax.fori_loop(0, CHUNKS, first, 0)
 
     for copy in kcopies:
         copy.wait_recv()
@@ -240,23 +245,21 @@
             )
         acc_last[...] += total
 
-    def exchange(phase, buffer, index, count, peer_of, source=None):
-        def of(k):
-            src = buffer.at[index] if source is None else source.at[lax.rem(index + k, count)]
-            return remote(src, buffer.at[index], asend.at[phase, k - 1], arecv.at[phase, k - 1], peer_of(k))
-
-        return [of(k) for k in range(1, count)]
+    def exchange(phase, buffer, index, count, peer_of):
+        return [
+            remote(buffer.at[index], buffer.at[index], asend.at[phase, k - 1], arecv.at[phase, k - 1], peer_of(k))
+            for k in range(1, count)
+        ]
 
     steps_lead = [
-        exchange(0, lead_y, gy, gy_n, y_peer, lead_own),
+        exchange(0, lead_y, gy, gy_n, y_peer),
         exchange(1, lead_z, zi, zg, z_peer),
         exchange(2, lead_x, xi, xg, x_peer),
-        exchange(3, lead_all, gy, gy_n, y_peer),
     ]
     steps_last = [
-        exchange(4, last_y, gy, gy_n, y_peer),
-        exchange(5, last_z, zi, zg, z_peer),
-        exchange(6, last_x, xi, xg, x_peer),
+        exchange(3, last_y, gy, gy_n, y_peer),
+        exchange(4, last_z, zi, zg, z_peer),
+        exchange(5, last_x, xi, xg, x_peer),
     ]
 
     def send(step):
@@ -291,28 +294,16 @@
     mirrored = jnp.concatenate([partial, jnp.zeros((128 - LEAD, 128), f32)], axis=0).T[LEAD : 2 * LEAD]
     lead_lane = lax.broadcasted_iota(jnp.int32, (LEAD, 128), 1)
     partial = jnp.where(lead_lane < LEAD, partial + pltpu.roll(partial, LEAD, 1), 0.0) + mirrored
-    for b in range(LEAD // 8):
-        lead_own[b] = partial[8 * b : 8 * b + 8]
-    lead_y[gy] = lead_own[gy]
+    lead_y[gy] = partial[: LEAD // 2] + pltpu.roll(partial[LEAD // 2 :], LEAD, 1)
     send(steps_lead[0])
 
     def beside(q):
         last_products(q)
 
-        @pl.when(q == 0)
+        @pl.when(q == CHUNKS - 2)
         def _():
             lead_z[zi] = collect(steps_lead[0], lead_y)
             send(steps_lead[1])
-
-        @pl.when(q == 1)
-        def _():
-            lead_x[xi] = collect(steps_lead[1], lead_z)
-            send(steps_lead[2])
-
-        @pl.when(q == 2)
-        def _():
-            lead_all[gy] = collect(steps_lead[2], lead_x)
-            send(steps_lead[3])
 
     loop(3, beside)
 
@@ -321,17 +312,16 @@
         [partial[:RHS, :COLS] + partial[:RHS, COLS:] + partial[RHS:, :COLS], jnp.zeros((RHS, 128 - COLS), f32)], axis=1
     )
     send(steps_last[0])
-    for copy in steps_lead[3]:
-        copy.wait_recv()
-    rows = eliminate_start([lead_all[b] * (1.0 / cells) for b in range(LEAD // 8)], LEAD)
-    rows = eliminate(rows, 0, 24)
     last_z[zi] = collect(steps_last[0], last_y)
     send(steps_last[1])
-    rows = eliminate(rows, 24, 48)
+    lead_x[xi] = collect(steps_lead[1], lead_z)
+    send(steps_lead[2])
     last_x[xi] = collect(steps_last[1], last_z)
     send(steps_last[2])
-    rows = eliminate(rows, 48, LEAD)
-    lead[...] = jnp.concatenate(eliminate_end(rows, LEAD), axis=0)
+    summed = collect(steps_lead[2], lead_x) * (1.0 / cells)
+    summed = jnp.concatenate([summed, pltpu.roll(summed, LEAD, 1)], axis=0)
+    rows, root = scale_start([summed[8 * b : 8 * b + 8] for b in range(LEAD // 8)], LEAD)
+    lead[...] = jnp.concatenate(scale_end(eliminate(rows, 0, LEAD), root, LEAD), axis=0)
     last_gram[...] = collect(steps_last[2], last_x) * (1.0 / cells)
 
     for copy in kcopies:
@@ -349,38 +339,63 @@
             copy.wait_send()
 
 
-def eliminate_start(blocks, size):
+def scale_start(blocks, size):
     lane = lax.broadcasted_iota(jnp.int32, (8, 128), 1)
     row = lax.broadcasted_iota(jnp.int32, (8, 128), 0)
-    return [
-        jnp.where(lane < size, block, jnp.where(lane - size == row + 8 * b, 1.0, 0.0).astype(f32))
-        for b, block in enumerate(blocks)
-    ]
+    scales = []
+    across = jnp.zeros((1, 128), f32)
+    root = jnp.zeros((1, 128), f32)
+    for b, block in enumerate(blocks):
+        on = lane == row + 8 * b
+        diagonal = jnp.sum(jnp.where(on, block, 0.0), axis=1, keepdims=True)
+        rooted = jnp.sqrt(diagonal)
+        scale = 1.0 / rooted
+        scales.append(scale)
+        across = across + jnp.sum(jnp.where(on, scale, 0.0), axis=0, keepdims=True)
+        root = root + jnp.sum(jnp.where(on, rooted, 0.0), axis=0, keepdims=True)
+    rows = [
+        jnp.where(lane < size, block * scale * across, jnp.where(lane - size == row + 8 * b, scale, 0.0))
+        for b, (block, scale) in enumerate(zip(blocks, scales))
+    ]
+    return rows, jnp.where(lane[:1] < size, root, 1.0)
 
 
 def eliminate(rows, begin, end):
     rows = list(rows)
-    sub = lax.broadcasted_iota(jnp.int32, (8, 1), 0)
-    for k in range(begin, end):
+    sub = lax.broadcasted_iota(jnp.int32, (8, 128), 0)
+
+    def along(block, k):
+        return jnp.broadcast_to(block[:, k : k + 1], (8, 128))
+
+    def down(block, k):
+        return jnp.broadcast_to(block[k : k + 1, :], (8, 128))
+
+    for k in range(begin, end, 2):
         b, s = divmod(k, 8)
-        pivot = rows[b][s : s + 1, :]
-        scaled = pivot * (1.0 / pivot[:, k : k + 1])
+        left = [along(block, k) for block in rows[b:]]
+        right = [along(block, k + 1) for block in rows[b:]]
+        first, second = down(rows[b], s), down(rows[b], s + 1)
+        a, c, d = down(left[0], s), down(right[0], s), down(right[0], s + 1)
+        inverse = 1.0 / (a * d - c * c)
+        p0 = (d * first - c * second) * inverse
+        p1 = (a * second - c * first) * inverse
+        inner = (c / a) * first
         for i in range(b, len(rows)):
-            column = rows[i][:, k : k + 1]
+            change = left[i - b] * p0 + right[i - b] * p1
             if i == b:
-                column = jnp.where(sub > s, column, 0.0)
-            rows[i] = rows[i] - column * scaled
+                change = jnp.where(sub > s + 1, change, jnp.where(sub == s + 1, inner, 0.0))
+            rows[i] = rows[i] - change
     return rows
 
 
-def eliminate_end(rows, size):
+def scale_end(rows, root, size):
     lane = lax.broadcasted_iota(jnp.int32, (8, 128), 1)
     row = lax.broadcasted_iota(jnp.int32, (8, 128), 0)
     done = []
     for b, block in enumerate(rows):
         diagonal = jnp.sum(jnp.where(lane == row + 8 * b, block, 0.0), axis=1, keepdims=True)
         block = jnp.where((lane >= row + 8 * b) & (lane - size <= row + 8 * b), block, 0.0)
-        done.append(block / jnp.sqrt(diagonal))
+        done.append(block * (1.0 / jnp.sqrt(diagonal)) * root)
     return done
 
 
@@ -396,8 +411,8 @@
     schur = last_gram[:, LEAD:COLS] - exact(cross, cross, NT)
     back = exact(cross, inverse, NN)
     padded = jnp.concatenate([schur, jnp.zeros((RHS, 128 - RHS), f32)], axis=1)
-    rows = eliminate_start([padded[:8], padded[8:]], RHS)
-    rows = eliminate_end(eliminate(rows, 0, RHS), RHS)
+    rows, root = scale_start([padded[:8], padded[8:]], RHS)
+    rows = scale_end(eliminate(rows, 0, RHS), root, RHS)
     corner = jnp.concatenate(rows, axis=0)
     corner_upper = corner[:, :RHS]
     corner_inverse = corner[:, RHS : 2 * RHS]
@@ -423,7 +438,7 @@
     low = whole - high
     weights = high + pltpu.roll(high, COLS, 1) + pltpu.roll(low, 2 * COLS, 1)
     weights = weights[:, : 3 * COLS].astype(bf16)
-    groups = 4
+    groups = 8
     per = NZ // groups
     copies = []
     for group in range(groups):
@@ -435,14 +450,14 @@
                     vh, vl = split(both)
                     q = jnp.dot(weights, jnp.concatenate([vh, vl, vh], axis=0), preferred_element_type=f32)
                     r = z * BX + 2 * h
-                    stage[pl.ds(r, COLS, stride=NZ * BX), :] = q[:, :BY]
-                    stage[pl.ds(r + 1, COLS, stride=NZ * BX), :] = q[:, BY:]
+                    stage[pl.ds(r, COLS, stride=PITCH), :] = q[:, :BY]
+                    stage[pl.ds(r + 1, COLS, stride=PITCH), :] = q[:, BY:]
             return carry
 
         lax.fori_loop(group * per // 4, (group + 1) * per // 4, block, 0)
         rows = pl.ds(group * per * BX, per * BX)
         copy = pltpu.make_async_copy(
-            stage.reshape(COLS, NZ * BX, BY).at[:, rows, :], out.at[:, rows, :], sems.at[group]
+            stage.reshape(COLS, PITCH, BY).at[:, rows, :], out.at[:, rows, :], sems.at[group]
         )
         copy.start()
         copies.append(copy)
@@ -472,11 +487,9 @@
         (NZ, BX, 6, HALF, BY),
         (LEAD, 2 * LEAD),
         (2 * RHS, 2 * COLS),
-        (LEAD // 8, 8, 128),
-        (gy_n, 8, 128),
-        (zg, 8, 128),
-        (xg, 8, 128),
-        (LEAD // 8, 8, 128),
+        (gy_n, LEAD // 2, 128),
+        (zg, LEAD // 2, 128),
+        (xg, LEAD // 2, 128),
         (gy_n, RHS, 128),
         (zg, RHS, 128),
         (xg, RHS, 128),
@@ -486,7 +499,7 @@
     ]
     dma = pltpu.SemaphoreType.DMA
     scratch += [dma((CHUNKS + 2,)), dma((4,)), dma((4,))]
-    scratch += [dma((S, CHUNKS, 2)) for _ in range(4)] + [dma((7, 8)), dma((7, 8))]
+    scratch += [dma((S, CHUNKS, 2)) for _ in range(4)] + [dma((6, 8)), dma((6, 8))]
     v, last_gram, lead = pl.pallas_call(
         functools.partial(basis_kernel, sizes, cells),
         out_shape=(
@@ -517,7 +530,7 @@
         ),
         in_specs=[vmem, vmem, vmem],
         out_specs=(hbm, vmem),
-        scratch_shapes=[pltpu.VMEM((COLS * NZ * BX, BY), f32), dma((4,))],
+        scratch_shapes=[pltpu.VMEM((COLS * PITCH, BY), f32), dma((8,))],
         compiler_params=pltpu.CompilerParams(vmem_limit_bytes=40 * 1024 * 1024),
         name="finish",
     )(v, last_gram, lead)

time: 72.5 us -> 57.8 us (0.80)
  Pallas kernels: 71.8 us -> 56.9 us
    pallas_call x1, Pallas kernels: 63.1 us -> 51.6 us  [per_device(): pl.pallas_call(functools.partial(basis_kernel, sizes, cells), out_shape=(...]
    pallas_call x1, Pallas kernels: 8.66 us -> 5.3 us  [per_device(): pl.pallas_call(finish_kernel, out_shape=(jax.ShapeDtypeStruct((COLS, NZ *...]
where the time goes in v2:
time: 57.8 us; the launch traced here: 57.6 us
  Pallas kernels  56.9 us (98%)
  between operations  0.64 us (1%)
    pallas_call x1, Pallas kernels, per_device(): pl.pallas_call(functools.partial(basis_kernel, sizes, cells), out_shape=(...  51.6 us
    pallas_call x1, Pallas kernels, per_device(): pl.pallas_call(finish_kernel, out_shape=(jax.ShapeDtypeStruct((COLS, NZ *...  5.3 us

profile of v2, /device:TPU:1, one launch (start us, length us, event | category | flops | bytes accessed | tf_op | source)
XLA Modules:
  0.0 57.6 jit_solution(15755078164195120083)
XLA Ops:
  0.6 51.6 %basis.1 = (f32[32,4,80,128]{3,2,1,0:T(8,128)S(1)}, f32[16,128]{1,0:T(8,128)S(1)}, f32[64,128]{1,0:T(8,128)S(1)}) custom-call(f32[16,128,128]{2,1,0:T(8,128)} %bitcast.4, s32[128,128]{1,0:T(8,128)} %bitcast.5, s32[8,128]{1,0:T(8,128)} %bitcast.6, f32[8]{0:T(128)} %perm.1), custom_call_target="tpu_custom_call" | custom-call | tf_op jit(solution)/shard_map/basis/pallas_call | solution.py:503
  52.3 5.3 %finish.1 = (f32[80,128,128]{2,1,0:T(8,128)}, f32[80,80]{1,0:T(8,128)}) custom-call(f32[32,4,80,128]{3,2,1,0:T(8,128)S(1)} %get-tuple-element.7.v, f32[16,128]{1,0:T(8,128)S(1)} %get-tuple-element.8.last_gram, f32[64,128]{1,0:T(8,128)S(1)} %get-tuple-element.9.lead), custom_call_target="tpu_custom_call" | custom-call | tf_op jit(solution)/shard_map/finish/pallas_call | solution.py:525

commit v3 on v2

--- a/solution.py
+++ b/solution.py
@@ -41,7 +41,7 @@
     sizes, cells,
     rs, labels_hbm, flags_hbm, perm,
     v, last_gram, lead,
-    stage, labels, flags, xl, xr, edge, yl, yr, kown, kxl, kxr, kyl, kyr, ct, cb,
+    stage, labels, flags, xl, xr, edge, yl, yr, kown, kedge, kxl, kxr, kyl, kyr, ct, cb,
     acc_lead, acc_last, lead_y, lead_z, lead_x, last_y, last_z, last_x,
     load_sem, ksend, krecv, xsend, xrecv, ysend, yrecv, asend, arecv,
 ):
@@ -67,18 +67,20 @@
     loads = [
         pltpu.make_async_copy(labels_hbm, labels, load_sem.at[CHUNKS]),
         pltpu.make_async_copy(flags_hbm, flags, load_sem.at[CHUNKS + 1]),
-    ] + [
-        pltpu.make_async_copy(
+    ]
+
+    def load_of(q):
+        return pltpu.make_async_copy(
             rs.at[:, pl.ds(q * ROWS, ROWS), :], stage.reshape(CHUNKS, RHS, ROWS, BY).at[q], load_sem.at[q]
         )
-        for q in range(CHUNKS)
-    ]
+
+    loads += [load_of(q) for q in range(CHUNKS)]
     for load in loads:
         load.start()
-    peers = [(right, gy), (left, gy)]
-    peers += [y_peer(k) for k in range(1, gy_n)]
-    peers += [z_peer(k) for k in range(1, zg)]
+    peers = [z_peer(k) for k in sorted(range(1, zg), key=lambda k: abs(k - zg // 2))]
+    peers += [y_peer(k) for k in sorted(range(1, gy_n), key=lambda k: abs(k - gy_n // 2))]
     peers += [x_peer(k) for k in range(1, xg)]
+    peers += [(right, gy), (left, gy)]
     barrier = pltpu.get_barrier_semaphore()
     for peer in peers:
         pl.semaphore_signal(barrier, inc=1, device_id=peer, device_id_type=MESH)
@@ -97,11 +99,16 @@
             src_ref=src, dst_ref=dst, send_sem=send, recv_sem=recv, device_id=peer, device_id_type=MESH
         )
 
+    wide_lane = lax.broadcasted_iota(jnp.int32, (NZ, BY), 1)
+    kends = jnp.zeros((NZ, BY), f32)
+    for x in range(BX):
+        kends = jnp.where(lax.div(wide_lane, 2) == x, pltpu.roll(kown[x], 2 * x + 1, 1), kends)
+    kedge[...] = kends
     kcopies = [
+        remote(kedge, kyl, ksend.at[2], krecv.at[2], (gx, above)),
+        remote(kedge, kyr, ksend.at[3], krecv.at[3], (gx, below)),
         remote(kown.at[BX - 1], kxl, ksend.at[0], krecv.at[0], (right, gy)),
         remote(kown.at[0], kxr, ksend.at[1], krecv.at[1], (left, gy)),
-        remote(kown, kyl, ksend.at[2], krecv.at[2], (gx, above)),
-        remote(kown, kyr, ksend.at[3], krecv.at[3], (gx, below)),
     ]
 
     def copies_of(j, q):
@@ -121,10 +128,8 @@
     def pack(value, rr, packed):
         return jnp.where(pair == rr, pltpu.roll(value, 2 * rr + 1, 1), packed)
 
-    for q in range(CHUNKS):
-        loads[2 + q].wait()
-
     def relayout(q, carry):
+        load_of(q).wait()
         packed = [jnp.zeros((HALF, BY), f32) for _ in range(2)]
         for s in range(LEVELS):
             for x in range(BX):
@@ -135,31 +140,32 @@
                     packed[h] = pack(value[h * HALF : (h + 1) * HALF], rr, packed[h])
         for h in range(2):
             edge[0, q, h] = packed[h]
-        return carry
-
-    def first(q, carry):
+
+        @pl.when(q == 0)
+        def _():
+            pl.semaphore_wait(barrier, len(peers))
+            for copy in kcopies:
+                copy.start()
+
         for copy in copies_of(0, q):
             copy.start()
         return carry
 
     lax.fori_loop(0, CHUNKS, relayout, 0)
-    pl.semaphore_wait(barrier, len(peers))
-    for copy in kcopies:
-        copy.start()
-    lax.fori_loop(0, CHUNKS, first, 0)
 
     for copy in kcopies:
         copy.wait_recv()
-    wide_lane = lax.broadcasted_iota(jnp.int32, (NZ, BY), 1)
     level = lax.broadcasted_iota(jnp.int32, (NZ, BY), 0)
+    merged = jnp.where(lax.rem(wide_lane, 2) == 1, pltpu.roll(kyl[...], 1, 1), pltpu.roll(kyr[...], BY - 1, 1))
     for x in range(BX):
         centre = kown[x]
         xm = kown[x - 1] if x > 0 else jnp.where(gx == 0, 0.0, kxl[...])
         xp = kown[x + 1] if x < BX - 1 else jnp.where(gx == gx_n - 1, 0.0, kxr[...])
-        from_below = jnp.where(gy == 0, 0.0, kyl[x])
-        from_above = jnp.where(gy == gy_n - 1, 0.0, kyr[x])
-        ym = jnp.where(wide_lane == 0, pltpu.roll(from_below, 1, 1), pltpu.roll(centre, 1, 1))
-        yp = jnp.where(wide_lane == BY - 1, pltpu.roll(from_above, BY - 1, 1), pltpu.roll(centre, BY - 1, 1))
+        ends = pltpu.roll(merged, BY - 1 - 2 * x, 1)
+        from_below = jnp.where(gy == 0, 0.0, ends)
+        from_above = jnp.where(gy == gy_n - 1, 0.0, ends)
+        ym = jnp.where(wide_lane == 0, from_below, pltpu.roll(centre, 1, 1))
+        yp = jnp.where(wide_lane == BY - 1, from_above, pltpu.roll(centre, BY - 1, 1))
         zm = jnp.where(level == 0, 0.0, pltpu.roll(centre, 1, 0))
         zp = jnp.where(level == NZ - 1, 0.0, pltpu.roll(centre, NZ - 1, 0))
         t = [harmonic(centre, other) for other in (xm, xp, ym, yp, zm, zp)]
@@ -481,8 +487,9 @@
         (BX, NZ, BY),
         (NZ, BY),
         (NZ, BY),
-        (BX, NZ, BY),
-        (BX, NZ, BY),
+        (NZ, BY),
+        (NZ, BY),
+        (NZ, BY),
         (6, BX, NZ, BY),
         (NZ, BX, 6, HALF, BY),
         (LEAD, 2 * LEAD),

time: 57.8 us -> 58 us (level)
  no operation moved by 1% of the time
where the time goes in v3:
time: 58 us; the launch traced here: 57.6 us
  Pallas kernels  57 us (98%)
  between operations  0.64 us (1%)
    pallas_call x1, Pallas kernels, per_device(): pl.pallas_call(functools.partial(basis_kernel, sizes, cells), out_shape=(...  51.7 us
    pallas_call x1, Pallas kernels, per_device(): pl.pallas_call(finish_kernel, out_shape=(jax.ShapeDtypeStruct((COLS, NZ *...  5.3 us

profile of v3, /device:TPU:1, one launch (start us, length us, event | category | flops | bytes accessed | tf_op | source)
XLA Modules:
  0.0 57.6 jit_solution(4981501045291288338)
XLA Ops:
  0.6 51.7 %basis.1 = (f32[32,4,80,128]{3,2,1,0:T(8,128)S(1)}, f32[16,128]{1,0:T(8,128)S(1)}, f32[64,128]{1,0:T(8,128)S(1)}) custom-call(f32[16,128,128]{2,1,0:T(8,128)} %bitcast.4, s32[128,128]{1,0:T(8,128)} %bitcast.5, s32[8,128]{1,0:T(8,128)} %bitcast.6, f32[8]{0:T(128)} %perm.1), custom_call_target="tpu_custom_call" | custom-call | tf_op jit(solution)/shard_map/basis/pallas_call | solution.py:510
  52.3 5.3 %finish.1 = (f32[80,128,128]{2,1,0:T(8,128)}, f32[80,80]{1,0:T(8,128)}) custom-call(f32[32,4,80,128]{3,2,1,0:T(8,128)S(1)} %get-tuple-element.7.v, f32[16,128]{1,0:T(8,128)S(1)} %get-tuple-element.8.last_gram, f32[64,128]{1,0:T(8,128)S(1)} %get-tuple-element.9.lead), custom_call_target="tpu_custom_call" | custom-call | tf_op jit(solution)/shard_map/finish/pallas_call | solution.py:532

commit v4 on v3

--- a/solution.py
+++ b/solution.py
@@ -42,7 +42,7 @@
     rs, labels_hbm, flags_hbm, perm,
     v, last_gram, lead,
     stage, labels, flags, xl, xr, edge, yl, yr, kown, kedge, kxl, kxr, kyl, kyr, ct, cb,
-    acc_lead, acc_last, lead_y, lead_z, lead_x, last_y, last_z, last_x,
+    acc_lead, acc_last, lead_own, lead_y, lead_z, lead_x, lead_all, last_y, last_z, last_x,
     load_sem, ksend, krecv, xsend, xrecv, ysend, yrecv, asend, arecv,
 ):
     gx_n, gy_n, zg, xg = sizes
@@ -251,21 +251,23 @@
             )
         acc_last[...] += total
 
-    def exchange(phase, buffer, index, count, peer_of):
-        return [
-            remote(buffer.at[index], buffer.at[index], asend.at[phase, k - 1], arecv.at[phase, k - 1], peer_of(k))
-            for k in range(1, count)
-        ]
+    def exchange(phase, buffer, index, count, peer_of, source=None):
+        def of(k):
+            src = buffer.at[index] if source is None else source.at[lax.rem(index + k, count)]
+            return remote(src, buffer.at[index], asend.at[phase, k - 1], arecv.at[phase, k - 1], peer_of(k))
+
+        return [of(k) for k in range(1, count)]
 
     steps_lead = [
-        exchange(0, lead_y, gy, gy_n, y_peer),
+        exchange(0, lead_y, gy, gy_n, y_peer, lead_own),
         exchange(1, lead_z, zi, zg, z_peer),
         exchange(2, lead_x, xi, xg, x_peer),
+        exchange(3, lead_all, gy, gy_n, y_peer),
     ]
     steps_last = [
-        exchange(3, last_y, gy, gy_n, y_peer),
-        exchange(4, last_z, zi, zg, z_peer),
-        exchange(5, last_x, xi, xg, x_peer),
+        exchange(4, last_y, gy, gy_n, y_peer),
+        exchange(5, last_z, zi, zg, z_peer),
+        exchange(6, last_x, xi, xg, x_peer),
     ]
 
     def send(step):
@@ -300,7 +302,9 @@
     mirrored = jnp.concatenate([partial, jnp.zeros((128 - LEAD, 128), f32)], axis=0).T[LEAD : 2 * LEAD]
     lead_lane = lax.broadcasted_iota(jnp.int32, (LEAD, 128), 1)
     partial = jnp.where(lead_lane < LEAD, partial + pltpu.roll(partial, LEAD, 1), 0.0) + mirrored
-    lead_y[gy] = partial[: LEAD // 2] + pltpu.roll(partial[LEAD // 2 :], LEAD, 1)
+    for b in range(LEAD // 8):
+        lead_own[b] = partial[8 * b : 8 * b + 8]
+    lead_y[gy] = lead_own[gy]
     send(steps_lead[0])
 
     def beside(q):
@@ -318,15 +322,17 @@
         [partial[:RHS, :COLS] + partial[:RHS, COLS:] + partial[RHS:, :COLS], jnp.zeros((RHS, 128 - COLS), f32)], axis=1
     )
     send(steps_last[0])
+    lead_x[xi] = collect(steps_lead[1], lead_z)
+    send(steps_lead[2])
     last_z[zi] = collect(steps_last[0], last_y)
     send(steps_last[1])
-    lead_x[xi] = collect(steps_lead[1], lead_z)
-    send(steps_lead[2])
+    lead_all[gy] = collect(steps_lead[2], lead_x)
+    send(steps_lead[3])
     last_x[xi] = collect(steps_last[1], last_z)
     send(steps_last[2])
-    summed = collect(steps_lead[2], lead_x) * (1.0 / cells)
-    summed = jnp.concatenate([summed, pltpu.roll(summed, LEAD, 1)], axis=0)
-    rows, root = scale_start([summed[8 * b : 8 * b + 8] for b in range(LEAD // 8)], LEAD)
+    for copy in steps_lead[3]:
+        copy.wait_recv()
+    rows, root = scale_start([lead_all[b] * (1.0 / cells) for b in range(LEAD // 8)], LEAD)
     lead[...] = jnp.concatenate(scale_end(eliminate(rows, 0, LEAD), root, LEAD), axis=0)
     last_gram[...] = collect(steps_last[2], last_x) * (1.0 / cells)
 
@@ -376,21 +382,38 @@
     def down(block, k):
         return jnp.broadcast_to(block[k : k + 1, :], (8, 128))
 
-    for k in range(begin, end, 2):
+    for k in range(begin, end, 4):
         b, s = divmod(k, 8)
-        left = [along(block, k) for block in rows[b:]]
-        right = [along(block, k + 1) for block in rows[b:]]
-        first, second = down(rows[b], s), down(rows[b], s + 1)
-        a, c, d = down(left[0], s), down(right[0], s), down(right[0], s + 1)
-        inverse = 1.0 / (a * d - c * c)
-        p0 = (d * first - c * second) * inverse
-        p1 = (a * second - c * first) * inverse
-        inner = (c / a) * first
+        columns = [[along(block, k + t) for block in rows[b:]] for t in range(4)]
+        r0, r1, r2, r3 = [down(rows[b], s + t) for t in range(4)]
+        p = {(t, u): down(columns[u][0], s + t) for t in range(4) for u in range(t, 4)}
+        i0 = 1.0 / p[0, 0]
+        l1, l2, l3 = p[0, 1] * i0, p[0, 2] * i0, p[0, 3] * i0
+        q11 = p[1, 1] - l1 * p[0, 1]
+        q12 = p[1, 2] - l1 * p[0, 2]
+        q13 = p[1, 3] - l1 * p[0, 3]
+        i1 = 1.0 / q11
+        m2, m3 = q12 * i1, q13 * i1
+        s22 = p[2, 2] - l2 * p[0, 2] - m2 * q12
+        s23 = p[2, 3] - l2 * p[0, 3] - m2 * q13
+        s33 = p[3, 3] - l3 * p[0, 3] - m3 * q13
+        i2 = 1.0 / s22
+        n3 = s23 * i2
+        i3 = 1.0 / (s33 - n3 * s23)
+        u1 = r1 - l1 * r0
+        u2 = r2 - l2 * r0 - m2 * u1
+        u3 = r3 - l3 * r0 - m3 * u1 - n3 * u2
+        z3 = i3 * u3
+        z2 = i2 * u2 - n3 * z3
+        z1 = i1 * u1 - m2 * z2 - m3 * z3
+        z0 = i0 * r0 - l1 * z1 - l2 * z2 - l3 * z3
         for i in range(b, len(rows)):
-            change = left[i - b] * p0 + right[i - b] * p1
+            c0, c1, c2, c3 = [column[i - b] for column in columns]
+            changed = rows[i] - (c0 * z0 + c1 * z1) - (c2 * z2 + c3 * z3)
             if i == b:
-                change = jnp.where(sub > s + 1, change, jnp.where(sub == s + 1, inner, 0.0))
-            rows[i] = rows[i] - change
+                kept = jnp.where(sub == s + 2, u2, jnp.where(sub == s + 3, u3, rows[i]))
+                changed = jnp.where(sub > s + 3, changed, jnp.where(sub == s + 1, u1, kept))
+            rows[i] = changed
     return rows
 
 
@@ -444,13 +467,13 @@
     low = whole - high
     weights = high + pltpu.roll(high, COLS, 1) + pltpu.roll(low, 2 * COLS, 1)
     weights = weights[:, : 3 * COLS].astype(bf16)
-    groups = 8
+    groups = 16
     per = NZ // groups
     copies = []
     for group in range(groups):
         def block(step, carry):
-            for s in range(4):
-                z = step * 4 + s
+            for s in range(2):
+                z = step * 2 + s
                 for h in range(2):
                     both = jnp.concatenate([v[z, 2 * h], v[z, 2 * h + 1]], axis=1)
                     vh, vl = split(both)
@@ -460,7 +483,7 @@
                     stage[pl.ds(r + 1, COLS, stride=PITCH), :] = q[:, BY:]
             return carry
 
-        lax.fori_loop(group * per // 4, (group + 1) * per // 4, block, 0)
+        lax.fori_loop(group * per // 2, (group + 1) * per // 2, block, 0)
         rows = pl.ds(group * per * BX, per * BX)
         copy = pltpu.make_async_copy(
             stage.reshape(COLS, PITCH, BY).at[:, rows, :], out.at[:, rows, :], sems.at[group]
@@ -494,9 +517,11 @@
         (NZ, BX, 6, HALF, BY),
         (LEAD, 2 * LEAD),
         (2 * RHS, 2 * COLS),
-        (gy_n, LEAD // 2, 128),
-        (zg, LEAD // 2, 128),
-        (xg, LEAD // 2, 128),
+        (LEAD // 8, 8, 128),
+        (gy_n, 8, 128),
+        (zg, 8, 128),
+        (xg, 8, 128),
+        (LEAD // 8, 8, 128),
         (gy_n, RHS, 128),
         (zg, RHS, 128),
         (xg, RHS, 128),
@@ -506,7 +531,7 @@
     ]
     dma = pltpu.SemaphoreType.DMA
     scratch += [dma((CHUNKS + 2,)), dma((4,)), dma((4,))]
-    scratch += [dma((S, CHUNKS, 2)) for _ in range(4)] + [dma((6, 8)), dma((6, 8))]
+    scratch += [dma((S, CHUNKS, 2)) for _ in range(4)] + [dma((7, 8)), dma((7, 8))]
     v, last_gram, lead = pl.pallas_call(
         functools.partial(basis_kernel, sizes, cells),
         out_shape=(
@@ -537,7 +562,7 @@
         ),
         in_specs=[vmem, vmem, vmem],
         out_specs=(hbm, vmem),
-        scratch_shapes=[pltpu.VMEM((COLS * PITCH, BY), f32), dma((8,))],
+        scratch_shapes=[pltpu.VMEM((COLS * PITCH, BY), f32), dma((16,))],
         compiler_params=pltpu.CompilerParams(vmem_limit_bytes=40 * 1024 * 1024),
         name="finish",
     )(v, last_gram, lead)

time: 58 us -> 59.7 us (1.029)
  Pallas kernels: 57 us -> 58.9 us
    pallas_call x1, Pallas kernels: 51.7 us -> 54 us  [per_device(): pl.pallas_call(functools.partial(basis_kernel, sizes, cells), out_shape=(...]
where the time goes in v4:
time: 59.7 us; the launch traced here: 59.6 us
  Pallas kernels  58.9 us (99%)
  between operations  0.64 us (1%)
    pallas_call x1, Pallas kernels, per_device(): pl.pallas_call(functools.partial(basis_kernel, sizes, cells), out_shape=(...  54 us
    pallas_call x1, Pallas kernels, per_device(): pl.pallas_call(finish_kernel, out_shape=(jax.ShapeDtypeStruct((COLS, NZ *...  4.91 us

profile of v4, /device:TPU:1, one launch (start us, length us, event | category | flops | bytes accessed | tf_op | source)
XLA Modules:
  0.0 59.6 jit_solution(17691334126011623176)
XLA Ops:
  0.6 54.0 %basis.1 = (f32[32,4,80,128]{3,2,1,0:T(8,128)S(1)}, f32[16,128]{1,0:T(8,128)S(1)}, f32[64,128]{1,0:T(8,128)S(1)}) custom-call(f32[16,128,128]{2,1,0:T(8,128)} %bitcast.4, s32[128,128]{1,0:T(8,128)} %bitcast.5, s32[8,128]{1,0:T(8,128)} %bitcast.6, f32[8]{0:T(128)} %perm.1), custom_call_target="tpu_custom_call" | custom-call | tf_op jit(solution)/shard_map/basis/pallas_call | solution.py:535
  54.7 4.9 %finish.1 = (f32[80,128,128]{2,1,0:T(8,128)}, f32[80,80]{1,0:T(8,128)}) custom-call(f32[32,4,80,128]{3,2,1,0:T(8,128)S(1)} %get-tuple-element.7.v, f32[16,128]{1,0:T(8,128)S(1)} %get-tuple-element.8.last_gram, f32[64,128]{1,0:T(8,128)S(1)} %get-tuple-element.9.lead), custom_call_target="tpu_custom_call" | custom-call | tf_op jit(solution)/shard_map/finish/pallas_call | solution.py:557

commit v5 on v4

--- a/solution.py
+++ b/solution.py
@@ -42,7 +42,7 @@
     rs, labels_hbm, flags_hbm, perm,
     v, last_gram, lead,
     stage, labels, flags, xl, xr, edge, yl, yr, kown, kedge, kxl, kxr, kyl, kyr, ct, cb,
-    acc_lead, acc_last, lead_own, lead_y, lead_z, lead_x, lead_all, last_y, last_z, last_x,
+    acc_lead, acc_last, lead_y, lead_z, lead_x, last_y, last_z, last_x,
     load_sem, ksend, krecv, xsend, xrecv, ysend, yrecv, asend, arecv,
 ):
     gx_n, gy_n, zg, xg = sizes
@@ -251,23 +251,21 @@
             )
         acc_last[...] += total
 
-    def exchange(phase, buffer, index, count, peer_of, source=None):
-        def of(k):
-            src = buffer.at[index] if source is None else source.at[lax.rem(index + k, count)]
-            return remote(src, buffer.at[index], asend.at[phase, k - 1], arecv.at[phase, k - 1], peer_of(k))
-
-        return [of(k) for k in range(1, count)]
+    def exchange(phase, buffer, index, count, peer_of):
+        return [
+            remote(buffer.at[index], buffer.at[index], asend.at[phase, k - 1], arecv.at[phase, k - 1], peer_of(k))
+            for k in range(1, count)
+        ]
 
     steps_lead = [
-        exchange(0, lead_y, gy, gy_n, y_peer, lead_own),
+        exchange(0, lead_y, gy, gy_n, y_peer),
         exchange(1, lead_z, zi, zg, z_peer),
         exchange(2, lead_x, xi, xg, x_peer),
-        exchange(3, lead_all, gy, gy_n, y_peer),
     ]
     steps_last = [
-        exchange(4, last_y, gy, gy_n, y_peer),
-        exchange(5, last_z, zi, zg, z_peer),
-        exchange(6, last_x, xi, xg, x_peer),
+        exchange(3, last_y, gy, gy_n, y_peer),
+        exchange(4, last_z, zi, zg, z_peer),
+        exchange(5, last_x, xi, xg, x_peer),
     ]
 
     def send(step):
@@ -302,9 +300,7 @@
     mirrored = jnp.concatenate([partial, jnp.zeros((128 - LEAD, 128), f32)], axis=0).T[LEAD : 2 * LEAD]
     lead_lane = lax.broadcasted_iota(jnp.int32, (LEAD, 128), 1)
     partial = jnp.where(lead_lane < LEAD, partial + pltpu.roll(partial, LEAD, 1), 0.0) + mirrored
-    for b in range(LEAD // 8):
-        lead_own[b] = partial[8 * b : 8 * b + 8]
-    lead_y[gy] = lead_own[gy]
+    lead_y[gy] = partial[: LEAD // 2] + pltpu.roll(partial[LEAD // 2 :], LEAD, 1)
     send(steps_lead[0])
 
     def beside(q):
@@ -322,17 +318,15 @@
         [partial[:RHS, :COLS] + partial[:RHS, COLS:] + partial[RHS:, :COLS], jnp.zeros((RHS, 128 - COLS), f32)], axis=1
     )
     send(steps_last[0])
+    last_z[zi] = collect(steps_last[0], last_y)
+    send(steps_last[1])
     lead_x[xi] = collect(steps_lead[1], lead_z)
     send(steps_lead[2])
-    last_z[zi] = collect(steps_last[0], last_y)
-    send(steps_last[1])
-    lead_all[gy] = collect(steps_lead[2], lead_x)
-    send(steps_lead[3])
     last_x[xi] = collect(steps_last[1], last_z)
     send(steps_last[2])
-    for copy in steps_lead[3]:
-        copy.wait_recv()
-    rows, root = scale_start([lead_all[b] * (1.0 / cells) for b in range(LEAD // 8)], LEAD)
+    summed = collect(steps_lead[2], lead_x) * (1.0 / cells)
+    summed = jnp.concatenate([summed, pltpu.roll(summed, LEAD, 1)], axis=0)
+    rows, root = scale_start([summed[8 * b : 8 * b + 8] for b in range(LEAD // 8)], LEAD)
     lead[...] = jnp.concatenate(scale_end(eliminate(rows, 0, LEAD), root, LEAD), axis=0)
     last_gram[...] = collect(steps_last[2], last_x) * (1.0 / cells)
 
@@ -517,11 +511,9 @@
         (NZ, BX, 6, HALF, BY),
         (LEAD, 2 * LEAD),
         (2 * RHS, 2 * COLS),
-        (LEAD // 8, 8, 128),
-        (gy_n, 8, 128),
-        (zg, 8, 128),
-        (xg, 8, 128),
-        (LEAD // 8, 8, 128),
+        (gy_n, LEAD // 2, 128),
+        (zg, LEAD // 2, 128),
+        (xg, LEAD // 2, 128),
         (gy_n, RHS, 128),
         (zg, RHS, 128),
         (xg, RHS, 128),
@@ -531,7 +523,7 @@
     ]
     dma = pltpu.SemaphoreType.DMA
     scratch += [dma((CHUNKS + 2,)), dma((4,)), dma((4,))]
-    scratch += [dma((S, CHUNKS, 2)) for _ in range(4)] + [dma((7, 8)), dma((7, 8))]
+    scratch += [dma((S, CHUNKS, 2)) for _ in range(4)] + [dma((6, 8)), dma((6, 8))]
     v, last_gram, lead = pl.pallas_call(
         functools.partial(basis_kernel, sizes, cells),
         out_shape=(

time: 59.7 us -> 56.7 us (0.950)
  Pallas kernels: 58.9 us -> 55.9 us
    pallas_call x1, Pallas kernels: 54 us -> 51 us  [per_device(): pl.pallas_call(functools.partial(basis_kernel, sizes, cells), out_shape=(...]
where the time goes in v5:
time: 56.7 us; the launch traced here: 56.6 us
  Pallas kernels  55.9 us (99%)
  between operations  0.64 us (1%)
    pallas_call x1, Pallas kernels, per_device(): pl.pallas_call(functools.partial(basis_kernel, sizes, cells), out_shape=(...  51 us
    pallas_call x1, Pallas kernels, per_device(): pl.pallas_call(finish_kernel, out_shape=(jax.ShapeDtypeStruct((COLS, NZ *...  4.91 us

profile of v5, /device:TPU:1, one launch (start us, length us, event | category | flops | bytes accessed | tf_op | source)
XLA Modules:
  0.0 56.6 jit_solution(222290523550347259)
XLA Ops:
  0.6 51.0 %basis.1 = (f32[32,4,80,128]{3,2,1,0:T(8,128)S(1)}, f32[16,128]{1,0:T(8,128)S(1)}, f32[64,128]{1,0:T(8,128)S(1)}) custom-call(f32[16,128,128]{2,1,0:T(8,128)} %bitcast.4, s32[128,128]{1,0:T(8,128)} %bitcast.5, s32[8,128]{1,0:T(8,128)} %bitcast.6, f32[8]{0:T(128)} %perm.1), custom_call_target="tpu_custom_call" | custom-call | tf_op jit(solution)/shard_map/basis/pallas_call | solution.py:527
  51.7 4.9 %finish.1 = (f32[80,128,128]{2,1,0:T(8,128)}, f32[80,80]{1,0:T(8,128)}) custom-call(f32[32,4,80,128]{3,2,1,0:T(8,128)S(1)} %get-tuple-element.7.v, f32[16,128]{1,0:T(8,128)S(1)} %get-tuple-element.8.last_gram, f32[64,128]{1,0:T(8,128)S(1)} %get-tuple-element.9.lead), custom_call_target="tpu_custom_call" | custom-call | tf_op jit(solution)/shard_map/finish/pallas_call | solution.py:549

commit v6 on v5

--- a/solution.py
+++ b/solution.py
@@ -19,6 +19,7 @@
 CHUNKS = NZ // LEVELS
 ROWS = LEVELS * BX
 PITCH = NZ * BX + 8
+PACKED = 8 + RHS * RHS // 128
 NT = (((1,), (1,)), ((), ()))
 NN = (((1,), (0,)), ((), ()))
 MESH = pl.DeviceIdType.MESH
@@ -251,33 +252,34 @@
             )
         acc_last[...] += total
 
-    def exchange(phase, buffer, index, count, peer_of):
+    def exchange(phase, buffer, index, count, peer_of, rows):
+        part = buffer.at[index, pl.ds(0, rows)]
         return [
-            remote(buffer.at[index], buffer.at[index], asend.at[phase, k - 1], arecv.at[phase, k - 1], peer_of(k))
-            for k in range(1, count)
+            remote(part, part, asend.at[phase, k - 1], arecv.at[phase, k - 1], peer_of(k))
+            for k in sorted(range(1, count), key=lambda k: abs(k - count // 2))
         ]
 
     steps_lead = [
-        exchange(0, lead_y, gy, gy_n, y_peer),
-        exchange(1, lead_z, zi, zg, z_peer),
-        exchange(2, lead_x, xi, xg, x_peer),
+        exchange(0, lead_y, gy, gy_n, y_peer, LEAD // 2),
+        exchange(1, lead_z, zi, zg, z_peer, LEAD // 2),
+        exchange(2, lead_x, xi, xg, x_peer, LEAD // 2),
     ]
     steps_last = [
-        exchange(3, last_y, gy, gy_n, y_peer),
-        exchange(4, last_z, zi, zg, z_peer),
-        exchange(5, last_x, xi, xg, x_peer),
+        exchange(3, last_y, gy, gy_n, y_peer, PACKED),
+        exchange(4, last_z, zi, zg, z_peer, PACKED),
+        exchange(5, last_x, xi, xg, x_peer, PACKED),
     ]
 
     def send(step):
         for copy in step:
             copy.start()
 
-    def collect(step, buffer):
+    def collect(step, buffer, rows):
         for copy in step:
             copy.wait_recv()
-        total = buffer[0]
+        total = buffer[0, :rows]
         for k in range(1, len(step) + 1):
-            total = total + buffer[k]
+            total = total + buffer[k, :rows]
         return total
 
     acc_lead[...] = jnp.zeros_like(acc_lead)
@@ -308,27 +310,26 @@
 
         @pl.when(q == CHUNKS - 2)
         def _():
-            lead_z[zi] = collect(steps_lead[0], lead_y)
+            lead_z[zi] = collect(steps_lead[0], lead_y, LEAD // 2)
             send(steps_lead[1])
 
     loop(3, beside)
 
     partial = acc_last[...]
-    last_y[gy] = jnp.concatenate(
-        [partial[:RHS, :COLS] + partial[:RHS, COLS:] + partial[RHS:, :COLS], jnp.zeros((RHS, 128 - COLS), f32)], axis=1
-    )
+    partial = partial[:RHS, :COLS] + partial[:RHS, COLS:] + partial[RHS:, :COLS]
+    last_y[gy, :PACKED] = pack_last(jnp.concatenate([partial, jnp.zeros((RHS, 128 - COLS), f32)], axis=1))
     send(steps_last[0])
-    last_z[zi] = collect(steps_last[0], last_y)
+    last_z[zi, :PACKED] = collect(steps_last[0], last_y, PACKED)
     send(steps_last[1])
-    lead_x[xi] = collect(steps_lead[1], lead_z)
+    lead_x[xi] = collect(steps_lead[1], lead_z, LEAD // 2)
     send(steps_lead[2])
-    last_x[xi] = collect(steps_last[1], last_z)
+    last_x[xi, :PACKED] = collect(steps_last[1], last_z, PACKED)
     send(steps_last[2])
-    summed = collect(steps_lead[2], lead_x) * (1.0 / cells)
+    summed = collect(steps_lead[2], lead_x, LEAD // 2) * (1.0 / cells)
     summed = jnp.concatenate([summed, pltpu.roll(summed, LEAD, 1)], axis=0)
     rows, root = scale_start([summed[8 * b : 8 * b + 8] for b in range(LEAD // 8)], LEAD)
     lead[...] = jnp.concatenate(scale_end(eliminate(rows, 0, LEAD), root, LEAD), axis=0)
-    last_gram[...] = collect(steps_last[2], last_x) * (1.0 / cells)
+    last_gram[...] = unpack_last(collect(steps_last[2], last_x, PACKED)) * (1.0 / cells)
 
     for copy in kcopies:
         copy.wait_send()
@@ -343,6 +344,34 @@
     for step in steps_lead + steps_last:
         for copy in step:
             copy.wait_send()
+
+
+def pack_last(block):
+    lane = lax.broadcasted_iota(jnp.int32, (8, 128), 1)
+    row = lax.broadcasted_iota(jnp.int32, (8, 128), 0)
+    packed = [jnp.where(lane < LEAD, block[:8], pltpu.roll(block[8:], LEAD, 1))]
+    for h in range(2):
+        corner = jnp.where(lane < RHS, pltpu.roll(block[8 * h : 8 * h + 8], LEAD, 1), 0.0)
+        spread = corner
+        for r in range(1, 8):
+            spread = jnp.where(row == r, pltpu.roll(corner, RHS * r, 1), spread)
+        packed.append(jnp.sum(spread, axis=0, keepdims=True))
+    return jnp.concatenate(packed, axis=0)
+
+
+def unpack_last(packed):
+    lane = lax.broadcasted_iota(jnp.int32, (8, 128), 1)
+    row = lax.broadcasted_iota(jnp.int32, (8, 128), 0)
+    block = []
+    for h in range(2):
+        side = packed[:8] if h == 0 else pltpu.roll(packed[:8], LEAD, 1)
+        line = jnp.broadcast_to(packed[8 + h : 9 + h], (8, 128))
+        corner = pltpu.roll(line, LEAD, 1)
+        for r in range(1, 8):
+            shift = (LEAD - RHS * r) % 128
+            corner = jnp.where(row == r, pltpu.roll(line, shift, 1) if shift else line, corner)
+        block.append(jnp.where(lane < LEAD, side, jnp.where(lane < COLS, corner, 0.0)))
+    return jnp.concatenate(block, axis=0)
 
 
 def scale_start(blocks, size):

time: 56.7 us -> 56.4 us (level)
  no operation moved by 1% of the time
where the time goes in v6:
time: 56.4 us; the launch traced here: 56.1 us
  Pallas kernels  55.5 us (98%)
  between operations  0.64 us (1%)
    pallas_call x1, Pallas kernels, per_device(): pl.pallas_call(functools.partial(basis_kernel, sizes, cells), out_shape=(...  50.6 us
    pallas_call x1, Pallas kernels, per_device(): pl.pallas_call(finish_kernel, out_shape=(jax.ShapeDtypeStruct((COLS, NZ *...  4.91 us

profile of v6, /device:TPU:1, one launch (start us, length us, event | category | flops | bytes accessed | tf_op | source)
XLA Modules:
  0.0 56.1 jit_solution(11756752324202872963)
XLA Ops:
  0.6 50.6 %basis.1 = (f32[32,4,80,128]{3,2,1,0:T(8,128)S(1)}, f32[16,128]{1,0:T(8,128)S(1)}, f32[64,128]{1,0:T(8,128)S(1)}) custom-call(f32[16,128,128]{2,1,0:T(8,128)} %bitcast.4, s32[128,128]{1,0:T(8,128)} %bitcast.5, s32[8,128]{1,0:T(8,128)} %bitcast.6, f32[8]{0:T(128)} %perm.1), custom_call_target="tpu_custom_call" | custom-call | tf_op jit(solution)/shard_map/basis/pallas_call | solution.py:556
  51.2 4.9 %finish.1 = (f32[80,128,128]{2,1,0:T(8,128)}, f32[80,80]{1,0:T(8,128)}) custom-call(f32[32,4,80,128]{3,2,1,0:T(8,128)S(1)} %get-tuple-element.7.v, f32[16,128]{1,0:T(8,128)S(1)} %get-tuple-element.8.last_gram, f32[64,128]{1,0:T(8,128)S(1)} %get-tuple-element.9.lead), custom_call_target="tpu_custom_call" | custom-call | tf_op jit(solution)/shard_map/finish/pallas_call | solution.py:578

commit v7 on v6

--- a/solution.py
+++ b/solution.py
@@ -40,11 +40,11 @@
 
 def basis_kernel(
     sizes, cells,
-    rs, labels_hbm, flags_hbm, perm,
+    rs, labels_hbm, flags_hbm, perm_hbm,
     v, last_gram, lead,
-    stage, labels, flags, xl, xr, edge, yl, yr, kown, kedge, kxl, kxr, kyl, kyr, ct, cb,
+    stage, labels, flags, perm, halo, edge, kown, kedge, khalo, ct, cb,
     acc_lead, acc_last, lead_y, lead_z, lead_x, last_y, last_z, last_x,
-    load_sem, ksend, krecv, xsend, xrecv, ysend, yrecv, asend, arecv,
+    load_sem, ksem, sent, arrived, asend, arecv,
 ):
     gx_n, gy_n, zg, xg = sizes
     gx = lax.axis_index("gx")
@@ -68,6 +68,7 @@
     loads = [
         pltpu.make_async_copy(labels_hbm, labels, load_sem.at[CHUNKS]),
         pltpu.make_async_copy(flags_hbm, flags, load_sem.at[CHUNKS + 1]),
+        pltpu.make_async_copy(perm_hbm, perm, load_sem.at[CHUNKS + 2]),
     ]
 
     def load_of(q):
@@ -86,8 +87,8 @@
     for peer in peers:
         pl.semaphore_signal(barrier, inc=1, device_id=peer, device_id_type=MESH)
 
-    loads[0].wait()
-    loads[1].wait()
+    for load in loads[:3]:
+        load.wait()
     for x in range(BX):
         label = labels[pl.ds(x, NZ, stride=BX), :]
         value = jnp.zeros((NZ, BY), f32)
@@ -106,20 +107,22 @@
         kends = jnp.where(lax.div(wide_lane, 2) == x, pltpu.roll(kown[x], 2 * x + 1, 1), kends)
     kedge[...] = kends
     kcopies = [
-        remote(kedge, kyl, ksend.at[2], krecv.at[2], (gx, above)),
-        remote(kedge, kyr, ksend.at[3], krecv.at[3], (gx, below)),
-        remote(kown.at[BX - 1], kxl, ksend.at[0], krecv.at[0], (right, gy)),
-        remote(kown.at[0], kxr, ksend.at[1], krecv.at[1], (left, gy)),
+        remote(kedge, khalo.at[2], ksem.at[0], ksem.at[1], (gx, above)),
+        remote(kedge, khalo.at[3], ksem.at[0], ksem.at[1], (gx, below)),
+        remote(kown.at[BX - 1], khalo.at[0], ksem.at[0], ksem.at[1], (right, gy)),
+        remote(kown.at[0], khalo.at[1], ksem.at[0], ksem.at[1], (left, gy)),
     ]
+    kall = remote(khalo, khalo, ksem.at[0], ksem.at[1], (right, gy))
 
     def copies_of(j, q):
         levels = pl.ds(q * LEVELS, LEVELS)
         plane = pl.ds(j * RHS, RHS)
+        here = halo.at[j, q]
         return [
-            remote(v.at[levels, BX - 1, plane, :], xl.at[j, q], xsend.at[j, q, 0], xrecv.at[j, q, 0], (right, gy)),
-            remote(v.at[levels, 0, plane, :], xr.at[j, q], xsend.at[j, q, 1], xrecv.at[j, q, 1], (left, gy)),
-            remote(edge.at[j, q], yl.at[j, q], ysend.at[j, q, 0], yrecv.at[j, q, 0], (gx, above)),
-            remote(edge.at[j, q], yr.at[j, q], ysend.at[j, q, 1], yrecv.at[j, q, 1], (gx, below)),
+            remote(v.at[levels, BX - 1, plane, :], here.at[pl.ds(0, LEVELS)], sent.at[0], arrived.at[j, q], (right, gy)),
+            remote(v.at[levels, 0, plane, :], here.at[pl.ds(LEVELS, LEVELS)], sent.at[1], arrived.at[j, q], (left, gy)),
+            remote(edge.at[j, q], here.at[2 * LEVELS], sent.at[2], arrived.at[j, q], (gx, above)),
+            remote(edge.at[j, q], here.at[2 * LEVELS + 1], sent.at[3], arrived.at[j, q], (gx, below)),
         ]
 
     lane = lax.broadcasted_iota(jnp.int32, (HALF, BY), 1)
@@ -140,7 +143,7 @@
                 for h in range(2):
                     packed[h] = pack(value[h * HALF : (h + 1) * HALF], rr, packed[h])
         for h in range(2):
-            edge[0, q, h] = packed[h]
+            edge[0, q, pl.ds(h * HALF, HALF)] = packed[h]
 
         @pl.when(q == 0)
         def _():
@@ -154,14 +157,13 @@
 
     lax.fori_loop(0, CHUNKS, relayout, 0)
 
-    for copy in kcopies:
-        copy.wait_recv()
+    kall.wait_recv()
     level = lax.broadcasted_iota(jnp.int32, (NZ, BY), 0)
-    merged = jnp.where(lax.rem(wide_lane, 2) == 1, pltpu.roll(kyl[...], 1, 1), pltpu.roll(kyr[...], BY - 1, 1))
+    merged = jnp.where(lax.rem(wide_lane, 2) == 1, pltpu.roll(khalo[2], 1, 1), pltpu.roll(khalo[3], BY - 1, 1))
     for x in range(BX):
         centre = kown[x]
-        xm = kown[x - 1] if x > 0 else jnp.where(gx == 0, 0.0, kxl[...])
-        xp = kown[x + 1] if x < BX - 1 else jnp.where(gx == gx_n - 1, 0.0, kxr[...])
+        xm = kown[x - 1] if x > 0 else jnp.where(gx == 0, 0.0, khalo[0])
+        xp = kown[x + 1] if x < BX - 1 else jnp.where(gx == gx_n - 1, 0.0, khalo[1])
         ends = pltpu.roll(merged, BY - 1 - 2 * x, 1)
         from_below = jnp.where(gy == 0, 0.0, ends)
         from_above = jnp.where(gy == gy_n - 1, 0.0, ends)
@@ -190,11 +192,15 @@
     lax.fori_loop(0, NZ // 8, spread, 0)
 
     def advance(j, q):
-        for copy in copies_of(j, q):
-            copy.wait_recv()
+        remote(halo.at[j, q], halo.at[j, q], sent.at[0], arrived.at[j, q], (right, gy)).wait_recv()
         base = q * LEVELS
         merged = [
-            jnp.where(odd, pltpu.roll(yl[j, q, h], 1, 1), pltpu.roll(yr[j, q, h], BY - 1, 1)) for h in range(2)
+            jnp.where(
+                odd,
+                pltpu.roll(halo[j, q, 2 * LEVELS, pl.ds(h * HALF, HALF), :], 1, 1),
+                pltpu.roll(halo[j, q, 2 * LEVELS + 1, pl.ds(h * HALF, HALF), :], BY - 1, 1),
+            )
+            for h in range(2)
         ]
         packed = [jnp.zeros((HALF, BY), f32) for _ in range(2)]
         for s in range(LEVELS):
@@ -208,8 +214,8 @@
                     here = pl.ds(j * RHS + h * HALF, HALF)
                     rows = pl.ds(h * HALF, HALF)
                     centre = v[z, x, here, :]
-                    xm = v[z, x - 1, here, :] if x > 0 else xl[j, q, s, rows, :]
-                    xp = v[z, x + 1, here, :] if x < BX - 1 else xr[j, q, s, rows, :]
+                    xm = v[z, x - 1, here, :] if x > 0 else halo[j, q, s, rows, :]
+                    xp = v[z, x + 1, here, :] if x < BX - 1 else halo[j, q, LEVELS + s, rows, :]
                     ends = pltpu.roll(merged[h], BY - 1 - 2 * rr, 1)
                     ym = jnp.where(lane == 0, ends, pltpu.roll(centre, 1, 1))
                     yp = jnp.where(lane == BY - 1, ends, pltpu.roll(centre, BY - 1, 1))
@@ -227,7 +233,7 @@
                         packed[h] = pack(value, rr, packed[h])
         if j < S - 1:
             for h in range(2):
-                edge[j + 1, q, h] = packed[h]
+                edge[j + 1, q, pl.ds(h * HALF, HALF)] = packed[h]
             for copy in copies_of(j + 1, q):
                 copy.start()
 
@@ -255,9 +261,15 @@
     def exchange(phase, buffer, index, count, peer_of, rows):
         part = buffer.at[index, pl.ds(0, rows)]
         return [
-            remote(part, part, asend.at[phase, k - 1], arecv.at[phase, k - 1], peer_of(k))
+            remote(part, part, asend.at[phase], arecv.at[phase], peer_of(k))
             for k in sorted(range(1, count), key=lambda k: abs(k - count // 2))
-        ]
+        ], remote(
+            buffer.at[pl.ds(0, count - 1), pl.ds(0, rows)],
+            buffer.at[pl.ds(0, count - 1), pl.ds(0, rows)],
+            asend.at[phase],
+            arecv.at[phase],
+            peer_of(1),
+        )
 
     steps_lead = [
         exchange(0, lead_y, gy, gy_n, y_peer, LEAD // 2),
@@ -271,14 +283,13 @@
     ]
 
     def send(step):
-        for copy in step:
+        for copy in step[0]:
             copy.start()
 
     def collect(step, buffer, rows):
-        for copy in step:
-            copy.wait_recv()
+        step[1].wait_recv()
         total = buffer[0, :rows]
-        for k in range(1, len(step) + 1):
+        for k in range(1, len(step[0]) + 1):
             total = total + buffer[k, :rows]
         return total
 
@@ -319,6 +330,11 @@
     partial = partial[:RHS, :COLS] + partial[:RHS, COLS:] + partial[RHS:, :COLS]
     last_y[gy, :PACKED] = pack_last(jnp.concatenate([partial, jnp.zeros((RHS, 128 - COLS), f32)], axis=1))
     send(steps_last[0])
+    kall.wait_send()
+    for i in range(2):
+        columns = halo.at[:, :, pl.ds(0, LEVELS)]
+        remote(columns, columns, sent.at[i], arrived.at[0, 0], (right, gy)).wait_send()
+        remote(edge, edge, sent.at[2 + i], arrived.at[0, 0], (right, gy)).wait_send()
     last_z[zi, :PACKED] = collect(steps_last[0], last_y, PACKED)
     send(steps_last[1])
     lead_x[xi] = collect(steps_lead[1], lead_z, LEAD // 2)
@@ -331,19 +347,8 @@
     lead[...] = jnp.concatenate(scale_end(eliminate(rows, 0, LEAD), root, LEAD), axis=0)
     last_gram[...] = unpack_last(collect(steps_last[2], last_x, PACKED)) * (1.0 / cells)
 
-    for copy in kcopies:
-        copy.wait_send()
-
-    def drain(q, carry):
-        for j in range(S):
-            for copy in copies_of(j, q):
-                copy.wait_send()
-        return carry
-
-    lax.fori_loop(0, CHUNKS, drain, 0)
     for step in steps_lead + steps_last:
-        for copy in step:
-            copy.wait_send()
+        step[1].wait_send()
 
 
 def pack_last(block):
@@ -525,17 +530,12 @@
         (CHUNKS * RHS * ROWS, BY),
         (NZ * BX, BY, jnp.int32),
         (2 * BX, BY, jnp.int32),
-        (S, CHUNKS, LEVELS, RHS, BY),
-        (S, CHUNKS, LEVELS, RHS, BY),
-        (S, CHUNKS, 2, HALF, BY),
-        (S, CHUNKS, 2, HALF, BY),
-        (S, CHUNKS, 2, HALF, BY),
+        None,
+        (S, CHUNKS, 2 * LEVELS + 2, RHS, BY),
+        (S, CHUNKS, RHS, BY),
         (BX, NZ, BY),
         (NZ, BY),
-        (NZ, BY),
-        (NZ, BY),
-        (NZ, BY),
-        (NZ, BY),
+        (4, NZ, BY),
         (6, BX, NZ, BY),
         (NZ, BX, 6, HALF, BY),
         (LEAD, 2 * LEAD),
@@ -548,11 +548,13 @@
         (xg, RHS, 128),
     ]
     scratch = [
-        pltpu.VMEM(shape[:-1], shape[-1]) if shape[-1] is jnp.int32 else pltpu.VMEM(shape, f32) for shape in scratch
+        pltpu.SMEM(region_perm.shape, f32) if shape is None
+        else pltpu.VMEM(shape[:-1], shape[-1]) if shape[-1] is jnp.int32
+        else pltpu.VMEM(shape, f32)
+        for shape in scratch
     ]
     dma = pltpu.SemaphoreType.DMA
-    scratch += [dma((CHUNKS + 2,)), dma((4,)), dma((4,))]
-    scratch += [dma((S, CHUNKS, 2)) for _ in range(4)] + [dma((6, 8)), dma((6, 8))]
+    scratch += [dma((CHUNKS + 3,)), dma((2,)), dma((4,)), dma((S, CHUNKS)), dma((6,)), dma((6,))]
     v, last_gram, lead = pl.pallas_call(
         functools.partial(basis_kernel, sizes, cells),
         out_shape=(
@@ -560,7 +562,7 @@
             pltpu.VMEM((RHS, 128), f32),
             pltpu.VMEM((LEAD, 2 * LEAD), f32),
         ),
-        in_specs=[hbm, hbm, hbm, pl.BlockSpec(memory_space=pltpu.SMEM)],
+        in_specs=[hbm, hbm, hbm, hbm],
         out_specs=(vmem, vmem, vmem),
         scratch_shapes=scratch,
         compiler_params=pltpu.CompilerParams(

time: 56.4 us -> 53.7 us (0.952)
  Pallas kernels: 55.5 us -> 52.9 us
    pallas_call x1, Pallas kernels: 50.6 us -> 48 us  [per_device(): pl.pallas_call(functools.partial(basis_kernel, sizes, cells), out_shape=(...]
where the time goes in v7:
time: 53.7 us; the launch traced here: 53.6 us
  Pallas kernels  52.9 us (99%)
  between operations  0.64 us (1%)
    pallas_call x1, Pallas kernels, per_device(): pl.pallas_call(functools.partial(basis_kernel, sizes, cells), out_shape=(...  48 us
    pallas_call x1, Pallas kernels, per_device(): pl.pallas_call(finish_kernel, out_shape=(jax.ShapeDtypeStruct((COLS, NZ *...  4.91 us

profile of v7, /device:TPU:1, one launch (start us, length us, event | category | flops | bytes accessed | tf_op | source)
XLA Modules:
  0.0 53.6 jit_solution(13607967574487857091)
XLA Ops:
  0.6 48.0 %basis.1 = (f32[32,4,80,128]{3,2,1,0:T(8,128)S(1)}, f32[16,128]{1,0:T(8,128)S(1)}, f32[64,128]{1,0:T(8,128)S(1)}) custom-call(f32[16,128,128]{2,1,0:T(8,128)} %bitcast.4, s32[128,128]{1,0:T(8,128)} %bitcast.5, s32[8,128]{1,0:T(8,128)} %bitcast.6, f32[8]{0:T(128)} %perm_hbm.1), custom_call_target="tpu_custom_call" | custom-call | tf_op jit(solution)/shard_map/basis/pallas_call | solution.py:558
  48.6 4.9 %finish.1 = (f32[80,128,128]{2,1,0:T(8,128)}, f32[80,80]{1,0:T(8,128)}) custom-call(f32[32,4,80,128]{3,2,1,0:T(8,128)S(1)} %get-tuple-element.7.v, f32[16,128]{1,0:T(8,128)S(1)} %get-tuple-element.8.last_gram, f32[64,128]{1,0:T(8,128)S(1)} %get-tuple-element.9.lead), custom_call_target="tpu_custom_call" | custom-call | tf_op jit(solution)/shard_map/finish/pallas_call | solution.py:580

commit v8 on v7

--- a/solution.py
+++ b/solution.py
@@ -460,7 +460,7 @@
     return lax.dot_general(a, b, dims, precision=lax.Precision.HIGHEST, preferred_element_type=f32)
 
 
-def finish_kernel(v, last_gram, lead, out, r_out, stage, sems):
+def finish_kernel(v, last_gram, lead, out, r_out, stage, r_stage, sems):
     upper = lead[:, :LEAD]
     inverse = lead[:, LEAD:]
     against = last_gram[:, :LEAD]
@@ -477,13 +477,15 @@
 
     tall = jnp.concatenate([cross, jnp.zeros((RHS, 128 - LEAD), f32)], axis=1)
     tall = jnp.concatenate([tall, jnp.zeros((128 - RHS, 128), f32)], axis=0).T[:LEAD, :RHS]
-    r_out[...] = jnp.concatenate(
+    r_stage[...] = jnp.concatenate(
         [
             jnp.concatenate([upper, tall], axis=1),
             jnp.concatenate([jnp.zeros((RHS, LEAD), f32), corner_upper], axis=1),
         ],
         axis=0,
     )
+    r_copy = pltpu.make_async_copy(r_stage, r_out, sems.at[0])
+    r_copy.start()
     whole = jnp.concatenate(
         [
             jnp.concatenate([inverse, jnp.zeros((LEAD, 256 - LEAD), f32)], axis=1),
@@ -497,7 +499,7 @@
     weights = weights[:, : 3 * COLS].astype(bf16)
     groups = 16
     per = NZ // groups
-    copies = []
+    planes = stage.reshape(COLS, PITCH, BY)
     for group in range(groups):
         def block(step, carry):
             for s in range(2):
@@ -513,13 +515,9 @@
 
         lax.fori_loop(group * per // 2, (group + 1) * per // 2, block, 0)
         rows = pl.ds(group * per * BX, per * BX)
-        copy = pltpu.make_async_copy(
-            stage.reshape(COLS, PITCH, BY).at[:, rows, :], out.at[:, rows, :], sems.at[group]
-        )
-        copy.start()
-        copies.append(copy)
-    for copy in copies:
-        copy.wait()
+        pltpu.make_async_copy(planes.at[:, rows, :], out.at[:, rows, :], sems.at[1]).start()
+    pltpu.make_async_copy(planes.at[:, pl.ds(0, NZ * BX), :], out, sems.at[1]).wait()
+    r_copy.wait()
 
 
 def per_device(sizes, cells, right_sides, region_labels, face_flags, region_perm):
@@ -584,8 +582,8 @@
             jax.ShapeDtypeStruct((COLS, COLS), f32),
         ),
         in_specs=[vmem, vmem, vmem],
-        out_specs=(hbm, vmem),
-        scratch_shapes=[pltpu.VMEM((COLS * PITCH, BY), f32), dma((16,))],
+        out_specs=(hbm, hbm),
+        scratch_shapes=[pltpu.VMEM((COLS * PITCH, BY), f32), pltpu.VMEM((COLS, COLS), f32), dma((2,))],
         compiler_params=pltpu.CompilerParams(vmem_limit_bytes=40 * 1024 * 1024),
         name="finish",
     )(v, last_gram, lead)

time: 53.7 us -> 53 us (0.987)
  Pallas kernels: 52.9 us -> 52.2 us
    pallas_call x1, Pallas kernels: 4.91 us -> 4.16 us  [per_device(): pl.pallas_call(finish_kernel, out_shape=(jax.ShapeDtypeStruct((COLS, NZ *...]
where the time goes in v8:
time: 53 us; the launch traced here: 52.8 us
  Pallas kernels  52.2 us (98%)
  between operations  0.64 us (1%)
    pallas_call x1, Pallas kernels, per_device(): pl.pallas_call(functools.partial(basis_kernel, sizes, cells), out_shape=(...  48 us
    pallas_call x1, Pallas kernels, per_device(): pl.pallas_call(finish_kernel, out_shape=(jax.ShapeDtypeStruct((COLS, NZ *...  4.16 us

profile of v8, /device:TPU:1, one launch (start us, length us, event | category | flops | bytes accessed | tf_op | source)
XLA Modules:
  0.0 52.8 jit_solution(18322032177682445045)
XLA Ops:
  0.6 48.0 %basis.1 = (f32[32,4,80,128]{3,2,1,0:T(8,128)S(1)}, f32[16,128]{1,0:T(8,128)S(1)}, f32[64,128]{1,0:T(8,128)S(1)}) custom-call(f32[16,128,128]{2,1,0:T(8,128)} %bitcast.4, s32[128,128]{1,0:T(8,128)} %bitcast.5, s32[8,128]{1,0:T(8,128)} %bitcast.6, f32[8]{0:T(128)} %perm_hbm.1), custom_call_target="tpu_custom_call" | custom-call | tf_op jit(solution)/shard_map/basis/pallas_call | solution.py:556
  48.6 4.2 %finish.1 = (f32[80,128,128]{2,1,0:T(8,128)}, f32[80,80]{1,0:T(8,128)}) custom-call(f32[32,4,80,128]{3,2,1,0:T(8,128)S(1)} %get-tuple-element.7.v, f32[16,128]{1,0:T(8,128)S(1)} %get-tuple-element.8.last_gram, f32[64,128]{1,0:T(8,128)S(1)} %get-tuple-element.9.lead), custom_call_target="tpu_custom_call" | custom-call | tf_op jit(solution)/shard_map/finish/pallas_call | solution.py:578

commit v9 on v8

--- a/solution.py
+++ b/solution.py
@@ -15,7 +15,7 @@
 BY = 128
 HALF = 8
 LEAD = RHS * S
-LEVELS = 8
+LEVELS = 4
 CHUNKS = NZ // LEVELS
 ROWS = LEVELS * BX
 PITCH = NZ * BX + 8

time: 53 us -> 52.4 us (0.989)
  no operation moved by 1% of the time
where the time goes in v9:
time: 52.4 us; the launch traced here: 52.3 us
  Pallas kernels  51.7 us (99%)
  between operations  0.64 us (1%)
    pallas_call x1, Pallas kernels, per_device(): pl.pallas_call(functools.partial(basis_kernel, sizes, cells), out_shape=(...  47.5 us
    pallas_call x1, Pallas kernels, per_device(): pl.pallas_call(finish_kernel, out_shape=(jax.ShapeDtypeStruct((COLS, NZ *...  4.16 us

profile of v9, /device:TPU:1, one launch (start us, length us, event | category | flops | bytes accessed | tf_op | source)
XLA Modules:
  0.0 52.3 jit_solution(6951213118601547)
XLA Ops:
  0.6 47.5 %basis.1 = (f32[32,4,80,128]{3,2,1,0:T(8,128)S(1)}, f32[16,128]{1,0:T(8,128)S(1)}, f32[64,128]{1,0:T(8,128)S(1)}) custom-call(f32[16,128,128]{2,1,0:T(8,128)} %bitcast.4, s32[128,128]{1,0:T(8,128)} %bitcast.5, s32[8,128]{1,0:T(8,128)} %bitcast.6, f32[8]{0:T(128)} %perm_hbm.1), custom_call_target="tpu_custom_call" | custom-call | tf_op jit(solution)/shard_map/basis/pallas_call | solution.py:556
  48.2 4.2 %finish.1 = (f32[80,128,128]{2,1,0:T(8,128)}, f32[80,80]{1,0:T(8,128)}) custom-call(f32[32,4,80,128]{3,2,1,0:T(8,128)S(1)} %get-tuple-element.7.v, f32[16,128]{1,0:T(8,128)S(1)} %get-tuple-element.8.last_gram, f32[64,128]{1,0:T(8,128)S(1)} %get-tuple-element.9.lead), custom_call_target="tpu_custom_call" | custom-call | tf_op jit(solution)/shard_map/finish/pallas_call | solution.py:578
